TPU v7x, 256 devices: a whole 4x4x8 slice. The times are simulated.
256 devices in a mesh: segment: 4 (over x), dp: 64 (over y, z, core).
Axes of the slice: x: 4, y: 4, z: 8, core: 2. Of those that a mesh axis runs over, the one named last changes fastest.
Arguments:
- items: bfloat16 [32768, 3584], P(('segment', 'dp')), may hold values from -36 to 36
- section_weights: bfloat16 [4, 3584, 1792], P('segment', 'dp'), may hold values from -0.09375 to 0.09375
- section_gains: float32 [4, 3584], P('segment'), may hold values from 0.25 to 1.75
- student_gain: float32 [3584], replicated, may hold values from 0.25 to 1.75
- adapter: bfloat16 [3584, 1024], replicated, may hold values from -0.09375 to 0.09375
- out_gain: float32 [1024], replicated, may hold values from 0.25 to 1.75
- assign: int32 [32768, 2], P(('segment', 'dp')), may hold values from 0 to 255, all different within a row; in each aligned block of 128 rows (0 to 127, 128 to 255, ...) at most 2 rows name the same one
- teacher_scores: bfloat16 [32768, 2, 128], P(('segment', 'dp')), may hold values from -12 to 412
- bank: bfloat16 [65536, 1024], P(('segment', 'dp')), may hold values from -12 to 12
- bank_bias: float32 [65536], P(('segment', 'dp')), may hold values from -8 to 408
- neg_index: int32 [256, 128], P(('segment', 'dp')), may hold values from 0 to 255
Outputs:
- emb_grad: float32 [32768, 1024], P(('segment', 'dp'))
- row_kl: bfloat16 [32768, 2], P(('segment', 'dp'))
- bank_grad: float32 [65536, 1024], P(('segment', 'dp'))
Inputs may be any that keep to these rules, and one draw needn't show every extreme that they name: `assign`: the 2 clusters of a row differ; among the rows of one device no cluster is named more than 2 times, and every cluster is named by some row.
All inputs are finite; a program needn't handle non-finite values.
Results may differ from a plain program's by a relative error of at most 0.035.
Values may be sent and summed in bfloat16 or wider, within the bound.
A program may use at most 128 MiB of HBM per device.

v0:
```python
import jax
import jax.numpy as jnp
from jax import lax
from jax.sharding import PartitionSpec as P

HD = 128


eps = 1e-06
temper = 4.0


def from_behind(block, axis, distance):
    devices = range(lax.axis_size(axis))
    route = [((i - distance) % len(devices), i) for i in devices]
    return lax.ppermute(block, axis, route)


def normalize(values, scale_row):
    values = values.astype(jnp.float32)
    return values * lax.rsqrt(jnp.mean(values * values, axis=-1, keepdims=True) + eps) * scale_row


def value_section(carried, weight, scale_row):
    normed = normalize(carried, scale_row).astype(jnp.bfloat16)
    values = jnp.dot(normed, weight, preferred_element_type=jnp.float32).astype(jnp.bfloat16)
    return jnp.pad(values, ((0, 0), (0, carried.shape[1] - weight.shape[1])))


def output_section(carried, weight, scale_row):
    value_width = weight.shape[1]
    row_count = carried.shape[0]
    head_values = (
        carried[:, :value_width].astype(jnp.float32).reshape(row_count, value_width // HD, HD)
    )
    head_values = head_values * lax.rsqrt(
        jnp.mean(head_values * head_values, axis=-1, keepdims=True) + eps
    )
    normed = head_values.reshape(row_count, value_width).astype(jnp.bfloat16)
    projected = lax.dot_general(
        normed, weight, (((1,), (1,)), ((), ())), preferred_element_type=jnp.float32
    )
    return (projected * scale_row).astype(jnp.bfloat16)


def run_ticks(carried, weight, scale_row, tick_count, advance):
    segments = lax.axis_size("segment")
    position = lax.axis_index("segment")
    is_output = position % 2 == 1

    def apply_section(current):
        return lax.cond(
            is_output,
            lambda held: output_section(held, weight, scale_row),
            lambda held: value_section(held, weight, scale_row),
            current,
        )

    for moment in range(tick_count):
        home_segment = (position - moment) % segments
        first_tick = (segments - home_segment) % segments
        is_due = moment == first_tick + position
        carried = lax.cond(is_due, apply_section, lambda held: held, carried)
        carried = advance(carried)
    return carried


def student(teacher_out, student_gain, adapter, out_gain):
    normed = normalize(teacher_out, student_gain).astype(jnp.bfloat16)
    raw_embed = jnp.dot(normed, adapter, preferred_element_type=jnp.float32)
    return normalize(raw_embed, out_gain).astype(jnp.bfloat16)


def shards(
    items,
    section_weights,
    section_gains,
    student_gain,
    adapter,
    out_gain,
    assign,
    teacher_scores,
    bank,
    bank_bias,
    neg_index,
):
    segments = lax.axis_size("segment")
    dp_count = lax.axis_size("dp")
    weight = lax.all_gather(section_weights[0], "dp", axis=0, tiled=True)
    scale_row = section_gains[0]
    carried = run_ticks(
        items, weight, scale_row, 2 * segments, lambda held: from_behind(held, "segment", 1)
    )
    embedding = student(carried, student_gain, adapter, out_gain)
    row_count = embedding.shape[0]
    pick_count = assign.shape[1]
    owners = segments * dp_count
    capacity = max(2, 2 * row_count * pick_count // owners)
    slot_count = owners * capacity
    pair_cluster = assign.reshape(-1)
    member = (pair_cluster[:, None] == jnp.arange(owners, dtype=jnp.int32)[None, :]).astype(
        jnp.int32
    )
    pair_rank = jnp.sum(jnp.cumsum(member, axis=0) * member, axis=1) - 1
    target = pair_cluster * capacity + pair_rank
    pick_map = target[None, :] == jnp.arange(slot_count, dtype=jnp.int32)[:, None]
    pair_map = pick_map.astype(jnp.bfloat16)
    row_map = jnp.any(pick_map.reshape(slot_count, row_count, pick_count), axis=2).astype(
        jnp.bfloat16
    )
    sent_embed = jnp.dot(row_map, embedding, preferred_element_type=jnp.float32).astype(
        jnp.bfloat16
    )
    sent_embed = sent_embed.reshape(segments, dp_count, capacity, -1)
    scores = teacher_scores.reshape(row_count * pick_count, -1)
    sent_scores = jnp.dot(pair_map, scores, preferred_element_type=jnp.float32).astype(jnp.bfloat16)
    sent_scores = sent_scores.reshape(segments, dp_count, capacity, -1)
    sent_valid = (
        jnp.sum(pick_map.astype(jnp.float32), axis=1)
        .astype(jnp.bfloat16)
        .reshape(segments, dp_count, capacity)
    )
    got_embed, got_scores, got_valid = (
        lax.all_to_all(
            lax.all_to_all(sent_embed, "segment", split_axis=0, concat_axis=0, tiled=True),
            "dp",
            split_axis=1,
            concat_axis=1,
            tiled=True,
        ),
        lax.all_to_all(
            lax.all_to_all(sent_scores, "segment", split_axis=0, concat_axis=0, tiled=True),
            "dp",
            split_axis=1,
            concat_axis=1,
            tiled=True,
        ),
        lax.all_to_all(
            lax.all_to_all(sent_valid, "segment", split_axis=0, concat_axis=0, tiled=True),
            "dp",
            split_axis=1,
            concat_axis=1,
            tiled=True,
        ),
    )
    neg_rows = neg_index[0]
    pool_size = bank.shape[0]
    embed_width = bank.shape[1]
    choose = neg_rows[:, None] == jnp.arange(pool_size, dtype=jnp.int32)[None, :]
    negatives = jnp.dot(
        choose.astype(jnp.bfloat16), bank, preferred_element_type=jnp.float32
    ).astype(jnp.bfloat16)
    offsets = jnp.dot(choose.astype(jnp.float32), bank_bias, precision=lax.Precision.HIGHEST)
    score_scale = temper * embed_width ** (-0.5)
    slot_embed = got_embed.reshape(slot_count, embed_width)
    slot_scores = got_scores.reshape(slot_count, -1).astype(jnp.float32)
    slot_valid = got_valid.reshape(slot_count).astype(jnp.float32)
    logits = (
        lax.dot_general(
            slot_embed, negatives, (((1,), (1,)), ((), ())), preferred_element_type=jnp.float32
        )
        * score_scale
        + offsets
    )
    student_log = jax.nn.log_softmax(logits, axis=-1)
    teacher_log = jax.nn.log_softmax(slot_scores, axis=-1)
    teacher_prob = jnp.exp(teacher_log)
    divergence = jnp.sum(teacher_prob * (teacher_log - student_log), axis=-1).astype(jnp.bfloat16)
    prob_gap = (slot_valid[:, None] * (jnp.exp(student_log) - teacher_prob)).astype(jnp.bfloat16)
    slot_grad = (
        jnp.dot(prob_gap, negatives, preferred_element_type=jnp.float32) * score_scale
    ).astype(jnp.bfloat16)
    neg_grad = (
        lax.dot_general(
            prob_gap, slot_embed, (((0,), (0,)), ((), ())), preferred_element_type=jnp.float32
        )
        * score_scale
    )
    bank_grad = lax.dot_general(
        choose.astype(jnp.float32),
        neg_grad,
        (((0,), (0,)), ((), ())),
        precision=lax.Precision.HIGHEST,
    )
    back_grad, back_kl = (
        lax.all_to_all(
            lax.all_to_all(
                slot_grad.reshape(segments, dp_count, capacity, embed_width),
                "segment",
                split_axis=0,
                concat_axis=0,
                tiled=True,
            ),
            "dp",
            split_axis=1,
            concat_axis=1,
            tiled=True,
        ),
        lax.all_to_all(
            lax.all_to_all(
                divergence.reshape(segments, dp_count, capacity),
                "segment",
                split_axis=0,
                concat_axis=0,
                tiled=True,
            ),
            "dp",
            split_axis=1,
            concat_axis=1,
            tiled=True,
        ),
    )
    home_grad = back_grad.reshape(slot_count, embed_width)
    emb_grad = lax.dot_general(
        row_map, home_grad, (((0,), (0,)), ((), ())), preferred_element_type=jnp.float32
    )
    row_kl = back_kl.reshape(slot_count)[target].reshape(row_count, pick_count)
    return (emb_grad, row_kl, bank_grad)


def solution(mesh):
    in_specs = (
        P(("segment", "dp"), None),
        P("segment", "dp", None),
        P("segment", None),
        P(),
        P(),
        P(),
        P(("segment", "dp"), None),
        P(("segment", "dp"), None, None),
        P(("segment", "dp"), None),
        P(("segment", "dp")),
        P(("segment", "dp"), None),
    )
    out_specs = (P(("segment", "dp"), None), P(("segment", "dp"), None), P(("segment", "dp"), None))
    return jax.shard_map(shards, mesh=mesh, in_specs=in_specs, out_specs=out_specs, check_vma=False)
```

profile of v0, /device:TPU:1, one launch (start us, length us, event | category | flops | bytes accessed | tf_op | source)
XLA Modules:
  0.0 557.3 jit_solution(9041586385270026705)
XLA Ops:
  7.2 2.2 copy.299
  9.5 95.9 %all-gather.3.cloned.1.call-done = bf16[1,3584,1792]{2,1,0:T(8,128)(2,1)} async-done(((bf16[1,56,1792]{2,1,0:T(8,128)(2,1)}), bf16[1,3584,1792]{2,1,0:T(8,128)(2,1)}) %all-gather.3.cloned.1.call-update) | async-done | bytes 12845072 | tf_op jit(solution)/shard_map/all_gather | solution.py:89
  105.4 10.0 %conditional.16 = (bf16[128,3584]{1,0:T(8,128)(2,1)}) conditional(s32[]{:T(128)} %convert_element_type.281, bf16[128,3584]{1,0:T(8,128)(2,1)} %copy.299, (pred[]{:T(512)}, bf16[128,3584]{1,0:T(8,128)(2,1)}, f32[1,3584]{1,0:T(1,128)S(1)}, bf16[3584,1792]{1,0:T(8,128)(2,1)}) %tuple.228), branch_computations={%region_5.6_spmd, %region_6.11_spmd} | conditional | flops 1647607936 | bytes 20230212 | solution.py:63
  105.4 1.5 copy.231
  107.0 8.4 %conditional = (bf16[128,3584]{1,0:T(8,128)(2,1)}) conditional(s32[]{:T(128)} %convert_element_type.192, (bf16[128,3584]{0,1:T(8,128)(2,1)S(1)}, f32[1,3584]{1,0:T(1,128)S(1)}, bf16[3584,1792]{1,0:T(8,128)(2,1)}) %tuple.79, (bf16[128,3584]{0,1:T(8,128)(2,1)S(1)}, bf16[3584,1792]{1,0:T(8,128)(2,1)}, f32[1,3584]{1,0:T(1,128)S(1)}) %tuple.80), branch_computations={%region_7.8_spmd, %region_9.10_spmd} | conditional | flops 1647607936 | bytes 18395150 | solution.py:52
  107.8 6.6 %convolution_convert_fusion = bf16[128,1792]{1,0:T(8,128)(2,1)S(1)} fusion(bf16[3584,1792]{1,0:T(8,128)(2,1)} %get-tuple-element.205, bf16[128,3584]{1,0:T(8,128)(2,1)S(1)} %copy.213, f32[3584]{0:T(1024)S(1)} %reduce, f32[128]{0:T(128)S(1)} %add_rsqrt_fusion), kind=kOutput, calls=%fused_computation.1 | convolution fusion | flops 1646231552 | bytes 14236160 | tf_op jit(solution)/shard_map/cond/branch_1_fun/cond/branch_0_fun/dot_general | solution.py:26
  115.4 1.5 copy.232
  117.1 22.9 %collective-permute-done = bf16[128,3584]{0,1:T(8,128)(2,1)S(1)} collective-permute-done((bf16[128,3584]{0,1:T(8,128)(2,1)S(1)}, bf16[128,3584]{0,1:T(8,128)(2,1)S(1)}, u32[]{:S(2)}, u32[]{:S(2)}) %collective-permute-start) | collective-permute-done | bytes 917536 | tf_op jit(solution)/shard_map/ppermute | solution.py:16
  139.9 15.9 %conditional.17 = (bf16[128,3584]{1,0:T(8,128)(2,1)}) conditional(s32[]{:T(128)} %convert_element_type.280, (bf16[128,3584]{0,1:T(8,128)(2,1)S(1)}) %tuple.174, (pred[]{:T(512)}, bf16[128,3584]{0,1:T(8,128)(2,1)S(1)}, f32[1,3584]{1,0:T(1,128)S(1)}, bf16[3584,1792]{1,0:T(8,128)(2,1)}) %tuple.229), branch_computations={%region_11.12_spmd, %region_12.17_spmd} | conditional | flops 1647607936 | bytes 18395204 | solution.py:63
  139.9 8.6 %conditional.1 = (bf16[128,3584]{1,0:T(8,128)(2,1)}) conditional(s32[]{:T(128)} %convert_element_type.199, (bf16[128,3584]{0,1:T(8,128)(2,1)S(1)}, f32[1,3584]{1,0:T(1,128)S(1)}, bf16[3584,1792]{1,0:T(8,128)(2,1)}) %tuple.81, (bf16[128,3584]{0,1:T(8,128)(2,1)S(1)}, bf16[3584,1792]{1,0:T(8,128)(2,1)}, f32[1,3584]{1,0:T(1,128)S(1)}) %tuple.82), branch_computations={%region_13.14_spmd, %region_15.16_spmd} | conditional | flops 1647607936 | bytes 18395150 | solution.py:52
  140.8 6.5 %convolution_convert_fusion.1 = bf16[128,1792]{1,0:T(8,128)(2,1)S(1)} fusion(bf16[3584,1792]{1,0:T(8,128)(2,1)} %get-tuple-element.229, bf16[128,3584]{1,0:T(8,128)(2,1)S(1)} %copy.214, f32[3584]{0:T(1024)S(1)} %reduce.2, f32[128]{0:T(128)S(1)} %add_rsqrt_fusion.2), kind=kOutput, calls=%fused_computation.16 | convolution fusion | flops 1646231552 | bytes 14236160 | tf_op jit(solution)/shard_map/cond/branch_1_fun/cond/branch_0_fun/dot_general | solution.py:26
  155.8 1.6 copy.234
  157.5 21.9 %collective-permute-done.1 = bf16[128,3584]{0,1:T(8,128)(2,1)S(1)} collective-permute-done((bf16[128,3584]{0,1:T(8,128)(2,1)S(1)}, bf16[128,3584]{0,1:T(8,128)(2,1)S(1)}, u32[]{:S(2)}, u32[]{:S(2)}) %collective-permute-start.1) | collective-permute-done | bytes 917536 | tf_op jit(solution)/shard_map/ppermute | solution.py:16
  179.4 8.4 %conditional.18 = (bf16[128,3584]{1,0:T(8,128)(2,1)}) conditional(s32[]{:T(128)} %convert_element_type.279, (bf16[128,3584]{0,1:T(8,128)(2,1)S(1)}) %tuple.175, (pred[]{:T(512)}, bf16[128,3584]{0,1:T(8,128)(2,1)S(1)}, f32[1,3584]{1,0:T(1,128)S(1)}, bf16[3584,1792]{1,0:T(8,128)(2,1)}) %tuple.230), branch_computations={%region_17.18_spmd, %region_18.23_spmd} | conditional | flops 1647607936 | bytes 18395204 | solution.py:63
  179.4 8.4 %conditional.2 = (bf16[128,3584]{1,0:T(8,128)(2,1)}) conditional(s32[]{:T(128)} %convert_element_type.206, (bf16[128,3584]{0,1:T(8,128)(2,1)S(1)}, f32[1,3584]{1,0:T(1,128)S(1)}, bf16[3584,1792]{1,0:T(8,128)(2,1)}) %tuple.83, (bf16[128,3584]{0,1:T(8,128)(2,1)S(1)}, bf16[3584,1792]{1,0:T(8,128)(2,1)}, f32[1,3584]{1,0:T(1,128)S(1)}) %tuple.84), branch_computations={%region_19.20_spmd, %region_21.22_spmd} | conditional | flops 1647607936 | bytes 18395150 | solution.py:52
  180.2 6.6 %convolution_convert_fusion.2 = bf16[128,1792]{1,0:T(8,128)(2,1)S(1)} fusion(bf16[3584,1792]{1,0:T(8,128)(2,1)} %get-tuple-element.239, bf16[128,3584]{1,0:T(8,128)(2,1)S(1)} %copy.215, f32[3584]{0:T(1024)S(1)} %reduce.4, f32[128]{0:T(128)S(1)} %add_rsqrt_fusion.4), kind=kOutput, calls=%fused_computation.31 | convolution fusion | flops 1646231552 | bytes 14236160 | tf_op jit(solution)/shard_map/cond/branch_1_fun/cond/branch_0_fun/dot_general | solution.py:26
  187.8 1.5 copy.236
  190.3 20.2 %collective-permute-done.2 = bf16[128,3584]{0,1:T(8,128)(2,1)S(1)} collective-permute-done((bf16[128,3584]{0,1:T(8,128)(2,1)S(1)}, bf16[128,3584]{0,1:T(8,128)(2,1)S(1)}, u32[]{:S(2)}, u32[]{:S(2)}) %collective-permute-start.2) | collective-permute-done | bytes 917536 | tf_op jit(solution)/shard_map/ppermute | solution.py:16
  210.5 16.2 %conditional.19 = (bf16[128,3584]{1,0:T(8,128)(2,1)}) conditional(s32[]{:T(128)} %convert_element_type.278, (bf16[128,3584]{0,1:T(8,128)(2,1)S(1)}) %tuple.176, (pred[]{:T(512)}, bf16[128,3584]{0,1:T(8,128)(2,1)S(1)}, f32[1,3584]{1,0:T(1,128)S(1)}, bf16[3584,1792]{1,0:T(8,128)(2,1)}) %tuple.231), branch_computations={%region_23.24_spmd, %region_24.29_spmd} | conditional | flops 1647607936 | bytes 18395204 | solution.py:63
  210.5 8.6 %conditional.3 = (bf16[128,3584]{1,0:T(8,128)(2,1)}) conditional(s32[]{:T(128)} %convert_element_type.213, (bf16[128,3584]{0,1:T(8,128)(2,1)S(1)}, f32[1,3584]{1,0:T(1,128)S(1)}, bf16[3584,1792]{1,0:T(8,128)(2,1)}) %tuple.85, (bf16[128,3584]{0,1:T(8,128)(2,1)S(1)}, bf16[3584,1792]{1,0:T(8,128)(2,1)}, f32[1,3584]{1,0:T(1,128)S(1)}) %tuple.86), branch_computations={%region_25.26_spmd, %region_27.28_spmd} | conditional | flops 1647607936 | bytes 18395150 | solution.py:52
  211.3 6.5 %convolution_convert_fusion.3 = bf16[128,1792]{1,0:T(8,128)(2,1)S(1)} fusion(bf16[3584,1792]{1,0:T(8,128)(2,1)} %get-tuple-element.249, bf16[128,3584]{1,0:T(8,128)(2,1)S(1)} %copy.216, f32[3584]{0:T(1024)S(1)} %reduce.6, f32[128]{0:T(128)S(1)} %add_rsqrt_fusion.6), kind=kOutput, calls=%fused_computation.46 | convolution fusion | flops 1646231552 | bytes 14236160 | tf_op jit(solution)/shard_map/cond/branch_1_fun/cond/branch_0_fun/dot_general | solution.py:26
  226.7 1.6 copy.238
  228.4 20.1 %collective-permute-done.3 = bf16[128,3584]{0,1:T(8,128)(2,1)S(1)} collective-permute-done((bf16[128,3584]{0,1:T(8,128)(2,1)S(1)}, bf16[128,3584]{0,1:T(8,128)(2,1)S(1)}, u32[]{:S(2)}, u32[]{:S(2)}) %collective-permute-start.3) | collective-permute-done | bytes 917536 | tf_op jit(solution)/shard_map/ppermute | solution.py:16
  248.4 1.3 conditional.20
  248.4 1.3 copy.261
  249.7 1.5 copy.240
  251.3 8.1 %collective-permute-start.4 = (bf16[128,3584]{0,1:T(8,128)(2,1)S(1)}, bf16[128,3584]{0,1:T(8,128)(2,1)S(1)}, u32[]{:S(2)}, u32[]{:S(2)}) collective-permute-start(bf16[128,3584]{0,1:T(8,128)(2,1)S(1)} %copy.240), channel_id=1, source_target_pairs={{192,0},{0,64},{64,128},{128,192},{193,1},{1,65},{65,129},{129,193... | collective-permute-start | bytes 2752520 | tf_op jit(solution)/shard_map/ppermute | solution.py:16
  259.3 17.0 %collective-permute-done.4 = bf16[128,3584]{0,1:T(8,128)(2,1)S(1)} collective-permute-done((bf16[128,3584]{0,1:T(8,128)(2,1)S(1)}, bf16[128,3584]{0,1:T(8,128)(2,1)S(1)}, u32[]{:S(2)}, u32[]{:S(2)}) %collective-permute-start.4) | collective-permute-done | bytes 917536 | tf_op jit(solution)/shard_map/ppermute | solution.py:16
  276.3 9.0 %conditional.21 = (bf16[128,3584]{1,0:T(8,128)(2,1)}) conditional(s32[]{:T(128)} %convert_element_type.276, (bf16[128,3584]{0,1:T(8,128)(2,1)S(1)}) %tuple.178, (pred[]{:T(512)}, bf16[128,3584]{0,1:T(8,128)(2,1)S(1)}, f32[1,3584]{1,0:T(1,128)S(1)}, bf16[3584,1792]{1,0:T(8,128)(2,1)}) %tuple.233), branch_computations={%region_35.36_spmd, %region_36.41_spmd} | conditional | flops 1647607936 | bytes 18395204 | solution.py:63
  285.3 1.6 copy.242
  286.8 1.4 collective-permute-start.5
  288.2 17.3 %collective-permute-done.5 = bf16[128,3584]{0,1:T(8,128)(2,1)S(1)} collective-permute-done((bf16[128,3584]{0,1:T(8,128)(2,1)S(1)}, bf16[128,3584]{0,1:T(8,128)(2,1)S(1)}, u32[]{:S(2)}, u32[]{:S(2)}) %collective-permute-start.5) | collective-permute-done | bytes 917536 | tf_op jit(solution)/shard_map/ppermute | solution.py:16
  305.5 1.3 conditional.22
  306.8 1.6 copy.244
  308.3 5.7 %collective-permute-start.6 = (bf16[128,3584]{0,1:T(8,128)(2,1)S(1)}, bf16[128,3584]{0,1:T(8,128)(2,1)S(1)}, u32[]{:S(2)}, u32[]{:S(2)}) collective-permute-start(bf16[128,3584]{0,1:T(8,128)(2,1)S(1)} %copy.244), channel_id=1, source_target_pairs={{192,0},{0,64},{64,128},{128,192},{193,1},{1,65},{65,129},{129,193... | collective-permute-start | bytes 2752520 | tf_op jit(solution)/shard_map/ppermute | solution.py:16
  315.1 25.3 %collective-permute-done.6 = bf16[128,3584]{0,1:T(8,128)(2,1)S(1)} collective-permute-done((bf16[128,3584]{0,1:T(8,128)(2,1)S(1)}, bf16[128,3584]{0,1:T(8,128)(2,1)S(1)}, u32[]{:S(2)}, u32[]{:S(2)}) %collective-permute-start.6) | collective-permute-done | bytes 917536 | tf_op jit(solution)/shard_map/ppermute | solution.py:16
  340.4 9.9 %conditional.23 = (bf16[128,3584]{1,0:T(8,128)(2,1)}) conditional(s32[]{:T(128)} %convert_element_type.274, (bf16[128,3584]{0,1:T(8,128)(2,1)S(1)}) %tuple.180, (pred[]{:T(512)}, bf16[128,3584]{0,1:T(8,128)(2,1)S(1)}, f32[1,3584]{1,0:T(1,128)S(1)}, bf16[3584,1792]{1,0:T(8,128)(2,1)}) %tuple.235), branch_computations={%region_47.48_spmd, %region_48.53_spmd} | conditional | flops 1647607936 | bytes 18395204 | solution.py:63
  351.4 3.9 all-to-all-start
  356.6 11.6 %all-to-all-done = bf16[4,64,2]{1,2,0:T(2,128)(2,1)S(1)} async-done(((bf16[4,64,2]{1,2,0:T(2,128)(2,1)}), bf16[4,64,2]{1,2,0:T(2,128)(2,1)S(1)}, u32[]{:S(2)}, u32[]{:S(2)}) %all-to-all-start) | async-done | bytes 1056 | tf_op jit(solution)/shard_map/all_to_all | solution.py:139
  368.9 12.5 %all-to-all-start.1 = ((bf16[4,64,2]{0,2,1:T(2,128)(2,1)}), bf16[4,64,2]{0,2,1:T(2,128)(2,1)S(1)}, u32[]{:S(2)}, u32[]{:S(2)}) async-start(bf16[4,64,2]{0,2,1:T(2,128)(2,1)} %copy.228), calls=%async_computation.1 | async-start | bytes 65536 | tf_op jit(solution)/shard_map/all_to_all | solution.py:138
  381.6 4.4 multiply_reduce_fusion
  386.0 4.6 all-to-all-done.1
  390.6 3.3 all-to-all-start.4
  395.7 3.0 all-to-all-done.4
  398.7 3.5 all-to-all-start.2
  403.0 12.5 %all-to-all-done.2 = bf16[4,64,2,1024]{3,2,1,0:T(2,128)(2,1)S(1)} async-done(((bf16[4,64,2,1024]{3,2,1,0:T(2,128)(2,1)}), bf16[4,64,2,1024]{3,2,1,0:T(2,128)(2,1)S(1)}, u32[]{:S(2)}, u32[]{:S(2)}) %all-to-all-start.2) | async-done | bytes 1048608 | tf_op jit(solution)/shard_map/all_to_all | solution.py:125
  415.5 8.1 %all-to-all-start.5 = ((bf16[4,64,2,128]{3,2,0,1:T(2,128)(2,1)}), bf16[4,64,2,128]{3,2,0,1:T(2,128)(2,1)S(1)}, u32[]{:S(2)}, u32[]{:S(2)}) async-start(bf16[4,64,2,128]{3,2,0,1:T(2,128)(2,1)} %copy.248), calls=%async_computation.5 | async-start | bytes 262144 | tf_op jit(solution)/shard_map/all_to_all | solution.py:131
  423.7 2.1 copy.246
  425.8 8.2 %all-to-all-done.5 = bf16[4,64,2,128]{3,2,0,1:T(2,128)(2,1)S(1)} async-done(((bf16[4,64,2,128]{3,2,0,1:T(2,128)(2,1)}), bf16[4,64,2,128]{3,2,0,1:T(2,128)(2,1)S(1)}, u32[]{:S(2)}, u32[]{:S(2)}) %all-to-all-start.5) | async-done | bytes 131104 | tf_op jit(solution)/shard_map/all_to_all | solution.py:131
  434.0 4.9 all-to-all-start.3
  440.5 27.0 %all-to-all-done.3 = bf16[4,64,2,1024]{3,2,0,1:T(2,128)(2,1)S(1)} async-done(((bf16[4,64,2,1024]{3,2,0,1:T(2,128)(2,1)}), bf16[4,64,2,1024]{3,2,0,1:T(2,128)(2,1)S(1)}, u32[]{:S(2)}, u32[]{:S(2)}) %all-to-all-start.3) | async-done | bytes 1048608 | tf_op jit(solution)/shard_map/all_to_all | solution.py:124
  470.3 3.2 all-to-all-start.8
  475.2 2.3 all-to-all-done.8
  477.5 3.5 all-to-all-start.6
  481.8 13.1 %all-to-all-done.6 = bf16[4,64,2,1024]{3,2,1,0:T(2,128)(2,1)S(1)} async-done(((bf16[4,64,2,1024]{3,2,1,0:T(2,128)(2,1)}), bf16[4,64,2,1024]{3,2,1,0:T(2,128)(2,1)S(1)}, u32[]{:S(2)}, u32[]{:S(2)}) %all-to-all-start.6) | async-done | bytes 1048608 | tf_op jit(solution)/shard_map/all_to_all | solution.py:187
  494.9 8.2 %all-to-all-start.9 = ((bf16[4,64,2]{0,2,1:T(2,128)(2,1)}), bf16[4,64,2]{0,2,1:T(2,128)(2,1)S(1)}, u32[]{:S(2)}, u32[]{:S(2)}) async-start(bf16[4,64,2]{0,2,1:T(2,128)(2,1)} %copy.255), calls=%async_computation.9 | async-start | bytes 65536 | tf_op jit(solution)/shard_map/all_to_all | solution.py:199
  503.1 2.2 copy.252
  505.3 7.0 %all-to-all-done.9 = bf16[4,64,2]{0,2,1:T(2,128)(2,1)S(1)} async-done(((bf16[4,64,2]{0,2,1:T(2,128)(2,1)}), bf16[4,64,2]{0,2,1:T(2,128)(2,1)S(1)}, u32[]{:S(2)}, u32[]{:S(2)}) %all-to-all-start.9) | async-done | bytes 1056 | tf_op jit(solution)/shard_map/all_to_all | solution.py:199
  512.3 4.7 all-to-all-start.7
  517.5 1.7 fusion.79
  519.9 1.9 gather_fusion
  522.6 23.0 %all-to-all-done.7 = bf16[4,64,2,1024]{3,2,0,1:T(2,128)(2,1)S(1)} async-done(((bf16[4,64,2,1024]{3,2,0,1:T(2,128)(2,1)}), bf16[4,64,2,1024]{3,2,0,1:T(2,128)(2,1)S(1)}, u32[]{:S(2)}, u32[]{:S(2)}) %all-to-all-start.7) | async-done | bytes 1048608 | tf_op jit(solution)/shard_map/all_to_all | solution.py:186
  545.6 1.7 copy.253
  547.3 1.5 reshape.310
  (106 shorter events, 28.8 us)
Async XLA Ops:
  7.2 432.0 %copy-start = (bf16[256,1024]{1,0:T(8,128)(2,1)S(1)}, bf16[256,1024]{1,0:T(8,128)(2,1)}, u32[]{:S(2)}) copy-start(bf16[256,1024]{1,0:T(8,128)(2,1)} %param.52) | copy-start | bytes 1572868
  7.2 98.2 %copy-start.1 = (f32[1,3584]{1,0:T(1,128)S(1)}, f32[1,3584]{1,0:T(1,128)}, u32[]{:S(2)}) copy-start(f32[1,3584]{1,0:T(1,128)} %param.46) | copy-start | bytes 43012
  7.2 98.2 %all-gather.3.cloned.1.call-start = ((), (), s32[]{:S(2)}) async-start(), calls=%async_computation.10 | async-start | bytes 13045760 | tf_op jit(solution)/shard_map/all_gather | solution.py:89
  116.9 23.0 %collective-permute-start = (bf16[128,3584]{0,1:T(8,128)(2,1)S(1)}, bf16[128,3584]{0,1:T(8,128)(2,1)S(1)}, u32[]{:S(2)}, u32[]{:S(2)}) collective-permute-start(bf16[128,3584]{0,1:T(8,128)(2,1)S(1)} %copy.232), channel_id=1, source_target_pairs={{192,0},{0,64},{64,128},{128,192},{193,1},{1,65},{65,129},{129,193... | collective-permute-start | bytes 2752520 | tf_op jit(solution)/shard_map/ppermute | solution.py:16
  157.4 22.0 %collective-permute-start.1 = (bf16[128,3584]{0,1:T(8,128)(2,1)S(1)}, bf16[128,3584]{0,1:T(8,128)(2,1)S(1)}, u32[]{:S(2)}, u32[]{:S(2)}) collective-permute-start(bf16[128,3584]{0,1:T(8,128)(2,1)S(1)} %copy.234), channel_id=1, source_target_pairs={{192,0},{0,64},{64,128},{128,192},{193,1},{1,65},{65,129},{129,193... | collective-permute-start | bytes 2752520 | tf_op jit(solution)/shard_map/ppermute | solution.py:16
  189.4 21.1 %collective-permute-start.2 = (bf16[128,3584]{0,1:T(8,128)(2,1)S(1)}, bf16[128,3584]{0,1:T(8,128)(2,1)S(1)}, u32[]{:S(2)}, u32[]{:S(2)}) collective-permute-start(bf16[128,3584]{0,1:T(8,128)(2,1)S(1)} %copy.236), channel_id=1, source_target_pairs={{192,0},{0,64},{64,128},{128,192},{193,1},{1,65},{65,129},{129,193... | collective-permute-start | bytes 2752520 | tf_op jit(solution)/shard_map/ppermute | solution.py:16
  228.3 20.2 %collective-permute-start.3 = (bf16[128,3584]{0,1:T(8,128)(2,1)S(1)}, bf16[128,3584]{0,1:T(8,128)(2,1)S(1)}, u32[]{:S(2)}, u32[]{:S(2)}) collective-permute-start(bf16[128,3584]{0,1:T(8,128)(2,1)S(1)} %copy.238), channel_id=1, source_target_pairs={{192,0},{0,64},{64,128},{128,192},{193,1},{1,65},{65,129},{129,193... | collective-permute-start | bytes 2752520 | tf_op jit(solution)/shard_map/ppermute | solution.py:16
  251.3 25.0 %collective-permute-start.4 = (bf16[128,3584]{0,1:T(8,128)(2,1)S(1)}, bf16[128,3584]{0,1:T(8,128)(2,1)S(1)}, u32[]{:S(2)}, u32[]{:S(2)}) collective-permute-start(bf16[128,3584]{0,1:T(8,128)(2,1)S(1)} %copy.240), channel_id=1, source_target_pairs={{192,0},{0,64},{64,128},{128,192},{193,1},{1,65},{65,129},{129,193... | collective-permute-start | bytes 2752520 | tf_op jit(solution)/shard_map/ppermute | solution.py:16
  286.8 18.7 %collective-permute-start.5 = (bf16[128,3584]{0,1:T(8,128)(2,1)S(1)}, bf16[128,3584]{0,1:T(8,128)(2,1)S(1)}, u32[]{:S(2)}, u32[]{:S(2)}) collective-permute-start(bf16[128,3584]{0,1:T(8,128)(2,1)S(1)} %copy.242), channel_id=1, source_target_pairs={{192,0},{0,64},{64,128},{128,192},{193,1},{1,65},{65,129},{129,193... | collective-permute-start | bytes 2752520 | tf_op jit(solution)/shard_map/ppermute | solution.py:16
  306.8 7.3 %copy-start.4 = (s32[128,2]{0,1:T(2,128)S(1)}, s32[128,2]{0,1:T(2,128)}, u32[]{:S(2)}) copy-start(s32[128,2]{0,1:T(2,128)} %param.50) | copy-start | bytes 3076
  308.3 32.1 %collective-permute-start.6 = (bf16[128,3584]{0,1:T(8,128)(2,1)S(1)}, bf16[128,3584]{0,1:T(8,128)(2,1)S(1)}, u32[]{:S(2)}, u32[]{:S(2)}) collective-permute-start(bf16[128,3584]{0,1:T(8,128)(2,1)S(1)} %copy.244), channel_id=1, source_target_pairs={{192,0},{0,64},{64,128},{128,192},{193,1},{1,65},{65,129},{129,193... | collective-permute-start | bytes 2752520 | tf_op jit(solution)/shard_map/ppermute | solution.py:16
  340.4 15.2 %copy-start.5 = (bf16[128,2,128]{2,1,0:T(2,128)(2,1)S(1)}, bf16[128,2,128]{2,1,0:T(2,128)(2,1)}, u32[]{:S(2)}) copy-start(bf16[128,2,128]{2,1,0:T(2,128)(2,1)} %param.51) | copy-start | bytes 196612
  350.3 31.3 %copy-start.6 = (f32[3584]{0:T(1024)S(1)}, f32[3584]{0:T(1024)}, u32[]{:S(2)}) copy-start(f32[3584]{0:T(1024)} %param.47) | copy-start | bytes 43012
  350.3 31.0 %collective-permute-start.7 = (bf16[128,3584]{1,0:T(8,128)(2,1)}, bf16[128,3584]{1,0:T(8,128)(2,1)S(1)}, u32[]{:S(2)}, u32[]{:S(2)}) collective-permute-start(bf16[128,3584]{1,0:T(8,128)(2,1)} %get-tuple-element.525), channel_id=1, source_target_pairs={{192,0},{0,64},{64,128},{128,192},{193,1},{1,65},{65,129},{129,193... | collective-permute-start | bytes 2752520 | tf_op jit(solution)/shard_map/ppermute | solution.py:16
  351.4 16.7 %all-to-all-start = ((bf16[4,64,2]{1,2,0:T(2,128)(2,1)}), bf16[4,64,2]{1,2,0:T(2,128)(2,1)S(1)}, u32[]{:S(2)}, u32[]{:S(2)}) async-start(bf16[4,64,2]{1,2,0:T(2,128)(2,1)} %copy.227), calls=%async_computation | async-start | bytes 4096 | tf_op jit(solution)/shard_map/all_to_all | solution.py:139
  368.9 21.7 %all-to-all-start.1 = ((bf16[4,64,2]{0,2,1:T(2,128)(2,1)}), bf16[4,64,2]{0,2,1:T(2,128)(2,1)S(1)}, u32[]{:S(2)}, u32[]{:S(2)}) async-start(bf16[4,64,2]{0,2,1:T(2,128)(2,1)} %copy.228), calls=%async_computation.1 | async-start | bytes 65536 | tf_op jit(solution)/shard_map/all_to_all | solution.py:138
  381.6 12.3 %copy-start.2 = (f32[1024]{0:T(1024)S(1)}, f32[1024]{0:T(1024)}, u32[]{:S(2)}) copy-start(f32[1024]{0:T(1024)} %param.49) | copy-start | bytes 12292
  390.6 8.1 %all-to-all-start.4 = ((bf16[4,64,2,128]{3,2,1,0:T(2,128)(2,1)}), bf16[4,64,2,128]{3,2,1,0:T(2,128)(2,1)S(1)}, u32[]{:S(2)}, u32[]{:S(2)}) async-start(bf16[4,64,2,128]{3,2,1,0:T(2,128)(2,1)} %bitcast.24), calls=%async_computation.4 | async-start | bytes 262144 | tf_op jit(solution)/shard_map/all_to_all | solution.py:132
  398.7 16.8 %all-to-all-start.2 = ((bf16[4,64,2,1024]{3,2,1,0:T(2,128)(2,1)}), bf16[4,64,2,1024]{3,2,1,0:T(2,128)(2,1)S(1)}, u32[]{:S(2)}, u32[]{:S(2)}) async-start(bf16[4,64,2,1024]{3,2,1,0:T(2,128)(2,1)} %reshape.305), calls=%async_computation.2 | async-start | bytes 2097152 | tf_op jit(solution)/shard_map/all_to_all | solution.py:125
  415.5 18.5 %all-to-all-start.5 = ((bf16[4,64,2,128]{3,2,0,1:T(2,128)(2,1)}), bf16[4,64,2,128]{3,2,0,1:T(2,128)(2,1)S(1)}, u32[]{:S(2)}, u32[]{:S(2)}) async-start(bf16[4,64,2,128]{3,2,0,1:T(2,128)(2,1)} %copy.248), calls=%async_computation.5 | async-start | bytes 262144 | tf_op jit(solution)/shard_map/all_to_all | solution.py:131
  423.7 15.3 %copy-start.3 = (s32[1,128]{1,0:T(1,128)S(1)}, s32[1,128]{1,0:T(1,128)}, u32[]{:S(2)}) copy-start(s32[1,128]{1,0:T(1,128)} %param.54) | copy-start | bytes 1540
  423.7 15.2 %copy-start.7 = (f32[256]{0:T(256)S(1)}, f32[256]{0:T(256)}, u32[]{:S(2)}) copy-start(f32[256]{0:T(256)} %param.53) | copy-start | bytes 3076
  434.0 33.4 %all-to-all-start.3 = ((bf16[4,64,2,1024]{3,2,0,1:T(2,128)(2,1)}), bf16[4,64,2,1024]{3,2,0,1:T(2,128)(2,1)S(1)}, u32[]{:S(2)}, u32[]{:S(2)}) async-start(bf16[4,64,2,1024]{3,2,0,1:T(2,128)(2,1)} %copy.246), calls=%async_computation.3 | async-start | bytes 2097152 | tf_op jit(solution)/shard_map/all_to_all | solution.py:124
  470.3 7.2 %all-to-all-start.8 = ((bf16[4,64,2]{1,2,0:T(2,128)(2,1)}), bf16[4,64,2]{1,2,0:T(2,128)(2,1)S(1)}, u32[]{:S(2)}, u32[]{:S(2)}) async-start(bf16[4,64,2]{1,2,0:T(2,128)(2,1)} %copy.254), calls=%async_computation.8 | async-start | bytes 4096 | tf_op jit(solution)/shard_map/all_to_all | solution.py:200
  477.5 17.4 %all-to-all-start.6 = ((bf16[4,64,2,1024]{3,2,1,0:T(2,128)(2,1)}), bf16[4,64,2,1024]{3,2,1,0:T(2,128)(2,1)S(1)}, u32[]{:S(2)}, u32[]{:S(2)}) async-start(bf16[4,64,2,1024]{3,2,1,0:T(2,128)(2,1)} %reshape.309), calls=%async_computation.6 | async-start | bytes 2097152 | tf_op jit(solution)/shard_map/all_to_all | solution.py:187
  494.9 17.4 %all-to-all-start.9 = ((bf16[4,64,2]{0,2,1:T(2,128)(2,1)}), bf16[4,64,2]{0,2,1:T(2,128)(2,1)S(1)}, u32[]{:S(2)}, u32[]{:S(2)}) async-start(bf16[4,64,2]{0,2,1:T(2,128)(2,1)} %copy.255), calls=%async_computation.9 | async-start | bytes 65536 | tf_op jit(solution)/shard_map/all_to_all | solution.py:199
  512.3 33.3 %all-to-all-start.7 = ((bf16[4,64,2,1024]{3,2,0,1:T(2,128)(2,1)}), bf16[4,64,2,1024]{3,2,0,1:T(2,128)(2,1)S(1)}, u32[]{:S(2)}, u32[]{:S(2)}) async-start(bf16[4,64,2,1024]{3,2,0,1:T(2,128)(2,1)} %copy.252), calls=%async_computation.7 | async-start | bytes 2097152 | tf_op jit(solution)/shard_map/all_to_all | solution.py:186
Sparse Core Ops, SparseCore 0:
  10.7 94.6 all-gather.2
where the time goes:
time: 565 us; the launch traced here: 557 us
  waiting for transfers between devices  353 us (62%)
  starting transfers between devices  72.4 us (13%)
  local copies, waits for them, and re-layouts  45.8 us (8%)
  matrix products  36.6 us (6%)
  loops' own time  31.8 us (6%)
  between operations  15.3 us (3%)
    ppermute x8, waiting for transfers between devices, from_behind(): return lax.ppermute(block, axis, route)  145 us
    all_gather x1, waiting for transfers between devices, shards(): weight = lax.all_gather(section_weights[0], 'dp', axis=0, tiled=True)  95.9 us
    another operation x8, loops' own time, run_ticks(): carried = lax.cond(is_due, apply_section, lambda held: held, carried)  31.2 us
    all_to_all x1, waiting for transfers between devices, shards(): lax.all_to_all(lax.all_to_all(sent_embed, 'segment', split_axis=0, concat...  27 us
    dot_general x4, matrix products, value_section(): jnp.dot(normed, weight, preferred_element_type=jnp.float32)  26.2 us
    all_to_all x1, waiting for transfers between devices, shards(): lax.all_to_all(lax.all_to_all(slot_grad.reshape(segments, dp_count, capac...  23 us
    ppermute x8, starting transfers between devices, from_behind(): return lax.ppermute(block, axis, route)  16.4 us
    all_to_all x1, waiting for transfers between devices, shards(): lax.all_to_all(slot_grad.reshape(segments, dp_count, capacity, embed_widt...  13.1 us
  transfers between devices with their start and end apart: 19, of which 18 were waited for; matrix products, arithmetic and copies ran while one was open for 4% of the time, Pallas kernels for 0%

commit v1 on v0

v1 whole, which is shorter than its diff:
```python
import functools

import jax
import jax.numpy as jnp
from jax import lax
from jax.experimental import pallas as pl
from jax.experimental.pallas import tpu as pltpu
from jax.sharding import PartitionSpec as P

HD = 128
MESH = pl.DeviceIdType.MESH

eps = 1e-06
temper = 4.0

SIZES = (4, 4, 8)
ORDERS = ((0, 1, 2), (1, 2, 0), (2, 0, 1))
PART_HEADS = (4, 5, 5)


def normalize(values, scale_row):
    values = values.astype(jnp.float32)
    return values * lax.rsqrt(jnp.mean(values * values, axis=-1, keepdims=True) + eps) * scale_row


def ring_plan():
    ready = {}
    hops = []
    free = {}
    todo = []
    for part, order in enumerate(ORDERS):
        for phase, axis in enumerate(order):
            for long_way in (True, False):
                steps = SIZES[axis] // 2 - (0 if long_way else 1)
                for step in range(steps):
                    todo.append((part, phase, long_way, step))
    blocks = lambda part, phase: PART_HEADS[part] * (
        1
        if phase == 0
        else SIZES[ORDERS[part][0]] * (1 if phase == 1 else SIZES[ORDERS[part][1]])
    )
    done = {}

    def start_of(hop):
        part, phase, long_way, step = hop
        if step > 0:
            return done.get((part, phase, long_way, step - 1))
        if phase == 0:
            return 0.0
        before = [h for h in todo_all if h[0] == part and h[1] == phase - 1]
        if any(h not in done for h in before):
            return None
        return max(done[h] for h in before)

    todo_all = list(todo)
    while todo:
        options = []
        for hop in todo:
            start = start_of(hop)
            if start is not None:
                axis = ORDERS[hop[0]][hop[1]]
                link = (axis, hop[2])
                options.append((max(start, free.get(link, 0.0)), hop, link))
        start, hop, link = min(options)
        share = 1.5 if hop[2] else 1.5
        finish = start + share * blocks(hop[0], hop[1]) + 1.0
        done[hop] = finish
        free[link] = start + share * blocks(hop[0], hop[1])
        todo.remove(hop)
        hops.append(hop)
    return sorted(hops, key=lambda hop: done[hop])


def gather_kernel(w_ref, out_ref, local_sem, send_sem, recv_sem, sib_send, sib_recv):
    x = lax.axis_index("segment")
    dp = lax.axis_index("dp")
    core = dp % 2
    z = (dp // 2) % SIZES[2]
    y = dp // (2 * SIZES[2])
    here = (x, y, z)

    def device(at, on):
        return (at[0], (at[1] * SIZES[2] + at[2]) * 2 + on)

    def moved(axis, by):
        at = list(here)
        at[axis] = (here[axis] + by + 2 * SIZES[axis]) % SIZES[axis]
        return tuple(at)

    sign = 1 - 2 * core
    sibling = device(here, 1 - core)

    mine = out_ref.at[x, y, z, core]
    own = pltpu.make_async_copy(w_ref, mine, local_sem)
    own.start()

    barrier = pltpu.get_barrier_semaphore()
    partners = [device(moved(axis, by), core) for axis in range(3) for by in (1, -1)] + [sibling]
    for partner in partners:
        pl.semaphore_signal(barrier, inc=1, device_id=partner, device_id_type=MESH)
    pl.semaphore_wait(barrier, len(partners))
    own.wait()

    starts = [sum(PART_HEADS[:part]) * HD for part in range(3)]

    def block(part, phase, place, on=core):
        order = ORDERS[part]
        at = list(here)
        at[order[phase]] = place
        for earlier in order[:phase]:
            at[earlier] = slice(None)
        return out_ref.at[
            at[0], at[1], at[2], on, :, pl.ds(starts[part], PART_HEADS[part] * HD)
        ]

    plan = ring_plan()
    number = {hop: i for i, hop in enumerate(plan)}
    sends = []

    def hop_copy(hop, sending):
        part, phase, long_way, step = hop
        axis = ORDERS[part][phase]
        size = SIZES[axis]
        toward = sign if long_way else -sign
        behind = step if sending else step + 1
        place = (here[axis] - toward * behind + 2 * size) % size
        held = block(part, phase, place)
        return pltpu.make_async_remote_copy(
            src_ref=held,
            dst_ref=held,
            send_sem=send_sem.at[number[hop]],
            recv_sem=recv_sem.at[number[hop]],
            device_id=device(moved(axis, toward), core),
            device_id_type=MESH,
        )

    def start(hop):
        copy = hop_copy(hop, True)
        copy.start()
        sends.append(copy)

    def to_sibling(index, held):
        copy = pltpu.make_async_remote_copy(
            src_ref=held,
            dst_ref=held,
            send_sem=sib_send.at[index],
            recv_sem=sib_recv.at[index],
            device_id=sibling,
            device_id_type=MESH,
        )
        copy.start()
        sends.append(copy)

    started = set()
    arrived = set()

    def start_ready():
        for hop in plan:
            if hop in started:
                continue
            part, phase, long_way, step = hop
            if step > 0:
                ready = (part, phase, long_way, step - 1) in arrived
            elif phase == 0:
                ready = True
            else:
                ready = all(h in arrived for h in plan if h[0] == part and h[1] == phase - 1)
            if ready:
                start(hop)
                started.add(hop)

    start_ready()
    to_sibling(len(plan), mine)
    for hop in plan:
        hop_copy(hop, False).wait_recv()
        arrived.add(hop)
        start_ready()
        part, phase, long_way, step = hop
        axis = ORDERS[part][phase]
        toward = sign if long_way else -sign
        place = (here[axis] - toward * (step + 1) + 2 * SIZES[axis]) % SIZES[axis]
        to_sibling(number[hop], block(part, phase, place))

    other = 1 - core
    for hop in plan:
        part, phase, long_way, step = hop
        axis = ORDERS[part][phase]
        toward = -sign if long_way else sign
        place = (here[axis] - toward * (step + 1) + 2 * SIZES[axis]) % SIZES[axis]
        held = block(part, phase, place, other)
        pltpu.make_async_remote_copy(
            src_ref=held,
            dst_ref=held,
            send_sem=sib_send.at[number[hop]],
            recv_sem=sib_recv.at[number[hop]],
            device_id=sibling,
            device_id_type=MESH,
        ).wait_recv()
    theirs = out_ref.at[x, y, z, other]
    pltpu.make_async_remote_copy(
        src_ref=theirs,
        dst_ref=theirs,
        send_sem=sib_send.at[len(plan)],
        recv_sem=sib_recv.at[len(plan)],
        device_id=sibling,
        device_id_type=MESH,
    ).wait_recv()
    for copy in sends:
        copy.wait_send()


def gather_weights(shard):
    rows, width = shard.shape
    hops = len(ring_plan())
    return pl.pallas_call(
        gather_kernel,
        out_shape=jax.ShapeDtypeStruct((*SIZES, 2, rows, width), shard.dtype),
        in_specs=[pl.BlockSpec(memory_space=pl.ANY)],
        out_specs=pl.BlockSpec(memory_space=pl.ANY),
        scratch_shapes=[
            pltpu.SemaphoreType.DMA,
            pltpu.SemaphoreType.DMA((hops,)),
            pltpu.SemaphoreType.DMA((hops,)),
            pltpu.SemaphoreType.DMA((hops + 1,)),
            pltpu.SemaphoreType.DMA((hops + 1,)),
        ],
        compiler_params=pltpu.CompilerParams(collective_id=0, has_side_effects=True),
        name="gather_weights",
    )(shard)


def value_section(carried, weight, scale_row):
    normed = normalize(carried, scale_row).astype(jnp.bfloat16)
    return jnp.dot(normed, weight, preferred_element_type=jnp.float32).astype(jnp.bfloat16)


def output_section(carried, weight, scale_row):
    rows, width = carried.shape
    heads = carried.astype(jnp.float32).reshape(rows, width // HD, HD)
    heads = heads * lax.rsqrt(jnp.mean(heads * heads, axis=-1, keepdims=True) + eps)
    normed = heads.reshape(rows, width).astype(jnp.bfloat16)
    projected = lax.dot_general(
        normed, weight, (((1,), (1,)), ((), ())), preferred_element_type=jnp.float32
    )
    return (projected * scale_row).astype(jnp.bfloat16)


def student(teacher_out, student_gain, adapter, out_gain):
    normed = normalize(teacher_out, student_gain).astype(jnp.bfloat16)
    raw_embed = jnp.dot(normed, adapter, preferred_element_type=jnp.float32)
    return normalize(raw_embed, out_gain).astype(jnp.bfloat16)


def shards(
    items,
    section_weights,
    section_gains,
    student_gain,
    adapter,
    out_gain,
    assign,
    teacher_scores,
    bank,
    bank_bias,
    neg_index,
):
    segments = lax.axis_size("segment")
    dp_count = lax.axis_size("dp")
    both = ("segment", "dp")
    owners = segments * dp_count

    gathered = gather_weights(section_weights[0])
    weights = gathered.reshape(segments, -1, section_weights.shape[2])
    gains = lax.all_gather(section_gains[0], "segment", axis=0)
    carried = items
    for section in range(segments):
        run = output_section if section % 2 else value_section
        carried = run(carried, weights[section], gains[section])
    embedding = student(carried, student_gain, adapter, out_gain)

    row_count = embedding.shape[0]
    pick_count = assign.shape[1]
    pair_count = row_count * pick_count
    capacity = max(2, 2 * pair_count // owners)
    slot_count = owners * capacity
    pair_cluster = assign.reshape(-1)
    same = pair_cluster[:, None] == pair_cluster[None, :]
    earlier = jnp.arange(pair_count)[:, None] > jnp.arange(pair_count)[None, :]
    pair_rank = jnp.sum((same & earlier).astype(jnp.int32), axis=1)
    target = pair_cluster * capacity + pair_rank
    pick_map = target[None, :] == jnp.arange(slot_count, dtype=jnp.int32)[:, None]
    pair_map = pick_map.astype(jnp.bfloat16)
    row_map = jnp.any(pick_map.reshape(slot_count, row_count, pick_count), axis=2).astype(
        jnp.bfloat16
    )
    sent_embed = jnp.dot(row_map, embedding, preferred_element_type=jnp.float32).astype(
        jnp.bfloat16
    )
    scores = teacher_scores.reshape(pair_count, -1)
    sent_scores = jnp.dot(pair_map, scores, preferred_element_type=jnp.float32).astype(jnp.bfloat16)
    valid = jnp.broadcast_to(
        jnp.sum(pick_map.astype(jnp.float32), axis=1, keepdims=True).astype(jnp.bfloat16),
        sent_scores.shape,
    )
    side = jnp.concatenate([sent_scores, valid], axis=1)

    def exchange(block):
        width = block.shape[1]
        block = block.reshape(owners, capacity * width)
        block = lax.all_to_all(block, both, split_axis=0, concat_axis=0, tiled=True)
        return block.reshape(slot_count, width)

    got_side = exchange(side)
    slot_embed = exchange(sent_embed)
    slot_scores = got_side[:, : scores.shape[1]].astype(jnp.float32)
    slot_valid = got_side[:, scores.shape[1]].astype(jnp.float32)

    neg_rows = neg_index[0]
    pool_size = bank.shape[0]
    embed_width = bank.shape[1]
    choose = neg_rows[:, None] == jnp.arange(pool_size, dtype=jnp.int32)[None, :]
    negatives = jnp.dot(
        choose.astype(jnp.bfloat16), bank, preferred_element_type=jnp.float32
    ).astype(jnp.bfloat16)
    offsets = jnp.dot(choose.astype(jnp.float32), bank_bias, precision=lax.Precision.HIGHEST)
    score_scale = temper * embed_width ** (-0.5)
    logits = (
        lax.dot_general(
            slot_embed, negatives, (((1,), (1,)), ((), ())), preferred_element_type=jnp.float32
        )
        * score_scale
        + offsets
    )
    student_log = jax.nn.log_softmax(logits, axis=-1)
    teacher_log = jax.nn.log_softmax(slot_scores, axis=-1)
    teacher_prob = jnp.exp(teacher_log)
    divergence = jnp.sum(teacher_prob * (teacher_log - student_log), axis=-1).astype(jnp.bfloat16)
    prob_gap = (slot_valid[:, None] * (jnp.exp(student_log) - teacher_prob)).astype(jnp.bfloat16)
    slot_grad = (
        jnp.dot(prob_gap, negatives, preferred_element_type=jnp.float32) * score_scale
    ).astype(jnp.bfloat16)
    neg_grad = (
        lax.dot_general(
            prob_gap, slot_embed, (((0,), (0,)), ((), ())), preferred_element_type=jnp.float32
        )
        * score_scale
    )
    bank_grad = lax.dot_general(
        choose.astype(jnp.float32),
        neg_grad,
        (((0,), (0,)), ((), ())),
        precision=lax.Precision.HIGHEST,
    )
    home_grad = exchange(slot_grad)
    home_kl = exchange(jnp.broadcast_to(divergence[:, None], (slot_count, HD)))[:, :1]
    emb_grad = lax.dot_general(
        row_map, home_grad, (((0,), (0,)), ((), ())), preferred_element_type=jnp.float32
    )
    row_kl = lax.dot_general(
        pair_map, home_kl, (((0,), (0,)), ((), ())), preferred_element_type=jnp.float32
    )
    row_kl = row_kl.astype(jnp.bfloat16).reshape(row_count, pick_count)
    return (emb_grad, row_kl, bank_grad)


def solution(mesh):
    in_specs = (
        P(("segment", "dp"), None),
        P("segment", "dp", None),
        P("segment", None),
        P(),
        P(),
        P(),
        P(("segment", "dp"), None),
        P(("segment", "dp"), None, None),
        P(("segment", "dp"), None),
        P(("segment", "dp")),
        P(("segment", "dp"), None),
    )
    out_specs = (P(("segment", "dp"), None), P(("segment", "dp"), None), P(("segment", "dp"), None))
    return jax.shard_map(shards, mesh=mesh, in_specs=in_specs, out_specs=out_specs, check_vma=False)
```

time: 565 us -> 528 us (0.935)
  waiting for transfers between devices: 353 us -> 56 us
  Pallas kernels: 0 us -> 262 us
  other arithmetic: 2.67 us -> 37.3 us
  loops' own time: 31.8 us -> 0 us
  starting transfers between devices: 72.4 us -> 49.4 us
  local copies, waits for them, and re-layouts: 45.8 us -> 67.2 us
  between operations: 15.3 us -> 1.33 us
  blocking collectives: 0 us -> 9.46 us
    pallas_call x0 -> x1, Pallas kernels: none -> 262 us  [gather_weights(): pl.pallas_call(gather_kernel, out_shape=jax.ShapeDtypeStruct((*SIZES, 2,...]
    ppermute x8 -> x0, waiting for transfers between devices: 145 us -> none  [from_behind(): return lax.ppermute(block, axis, route)]
    all_gather x1 -> x0, waiting for transfers between devices: 95.9 us -> none  [shards(): weight = lax.all_gather(section_weights[0], 'dp', axis=0, tiled=True)]
    all_to_all x10 -> x4, waiting for transfers between devices: 112 us -> 56 us  [exchange(): block = lax.all_to_all(block, both, split_axis=0, concat_axis=0, tiled=True)]
    all_to_all x0 -> x8, other arithmetic: none -> 35.3 us  [exchange(): block = lax.all_to_all(block, both, split_axis=0, concat_axis=0, tiled=True)]
    another operation x12 -> x0, loops' own time: 31.8 us -> none  [the longest x8 31.2 us: run_ticks(): carried = lax.cond(is_due, apply_section, lambda held: held, carried)]
    slice x0 -> x4, local copies, waits for them, and re-layouts: none -> 31.3 us  [the longest x2 31.2 us: shards(): carried = run(carried, weights[section], gains[section])]
    dot_general x0 -> x3, matrix products: none -> 18.4 us  [the longest x2 18.2 us: output_section(): lax.dot_general(normed, weight, (((1,), (1,)), ((), ())), preferred_eleme...]
  transfers between devices with their start and end apart: 19 -> 4, of which waited for: 18 -> 2; matrix products, arithmetic and copies ran while one was open for 4% -> 18% of each run, Pallas kernels for 0% -> 50%
where the time goes in v1:
time: 528 us; the launch traced here: 522 us
  Pallas kernels  262 us (50%)
  local copies, waits for them, and re-layouts  67.2 us (13%)
  waiting for transfers between devices  56 us (11%)
  starting transfers between devices  49.4 us (9%)
  matrix products  39.4 us (7%)
  other arithmetic  37.3 us (7%)
  blocking collectives  9.46 us (2%)
    pallas_call x1, Pallas kernels, gather_weights(): pl.pallas_call(gather_kernel, out_shape=jax.ShapeDtypeStruct((*SIZES, 2,...  262 us
    all_to_all x4, waiting for transfers between devices, exchange(): block = lax.all_to_all(block, both, split_axis=0, concat_axis=0, tiled=True)  56 us
    all_to_all x4, starting transfers between devices, exchange(): block = lax.all_to_all(block, both, split_axis=0, concat_axis=0, tiled=True)  49.4 us
    all_to_all x8, other arithmetic, exchange(): block = lax.all_to_all(block, both, split_axis=0, concat_axis=0, tiled=True)  35.3 us
    slice x2, local copies, waits for them, and re-layouts, shards(): carried = run(carried, weights[section], gains[section])  31.2 us
    unnamed x30, local copies, waits for them, and re-layouts  20.8 us
    dot_general x2, matrix products, output_section(): lax.dot_general(normed, weight, (((1,), (1,)), ((), ())), preferred_eleme...  18.2 us
  transfers between devices with their start and end apart: 4, of which 2 were waited for; matrix products, arithmetic and copies ran while one was open for 18% of the time, Pallas kernels for 50%

profile of v1, /device:TPU:1, one launch (start us, length us, event | category | flops | bytes accessed | tf_op | source)
XLA Modules:
  0.0 522.5 jit_solution(6662269220271799293)
XLA Ops:
  0.6 0.8 copy.79
  1.5 0.1 eq.50
  1.6 0.2 convert_reduce_fusion.3
  1.8 0.1 convert_reduce_fusion
  2.0 1.1 convolution_convert_fusion.4
  3.1 0.1 copy.81
  3.3 0.1 all_to_all.32
  3.4 0.5 broadcast.123
  3.9 2.2 reduce.16
  6.2 0.8 reshape.190
  6.9 15.7 %all-to-all-start = ((bf16[256,2,256]{2,1,0:T(2,128)(2,1)}), bf16[256,2,256]{2,1,0:T(2,128)(2,1)S(1)}, u32[]{:S(2)}, u32[]{:S(2)}) async-start(bf16[256,2,256]{2,1,0:T(2,128)(2,1)} %reshape.190), calls=%async_computation | async-start | bytes 524288 | tf_op jit(solution)/shard_map/all_to_all | solution.py:310
  22.6 0.8 reduce_sum.93
  23.4 262.4 %gather_weights.1 = bf16[4,4,8,2,56,1792]{5,4,3,2,1,0:T(8,128)(2,1)} custom-call(bf16[56,1792]{1,0:T(8,128)(2,1)} %bitcast.45), custom_call_target="tpu_custom_call" | custom-call | tf_op jit(solution)/shard_map/gather_weights/pallas_call | solution.py:215
  285.8 30.5 %fusion.39 = (bf16[1,4,8,2,56,1792]{5,4,3,2,1,0:T(8,128)(2,1)S(1)}, bf16[1,4,8,2,56,1792]{5,4,3,2,1,0:T(8,128)(2,1)}, bf16[1,4,8,2,56,1792]{5,4,3,2,1,0:T(8,128)(2,1)}, bf16[1,4,8,2,56,1792]{5,4,3,2,1,0:T(8,128)(2,1)}) fusion(bf16[4,4,8,2,56,1792]{5,4,3,2,1,0:T(8,128)(2,1)} %gather_weights.1), kind=kLoop, calls=%fused_computation.83 | loop fusion | bytes 102760448 | tf_op jit(solution)/shard_map/slice | solution.py:278
  316.2 9.5 %all-gather = f32[4,1,3584]{2,1,0:T(1,128)S(1)} all-gather(f32[1,1,3584]{2,1,0:T(1,128)S(1)} %bitcast.46), channel_id=1, replica_groups=mesh['segment'=4,'dp'=64] {'segment'}, dimensions={0}, use_global_device_ids=true | all-gather | bytes 71680 | tf_op jit(solution)/shard_map/all_gather | solution.py:274
  325.7 0.7 slice_reduce_fusion.2
  326.4 0.3 fusion.6
  326.7 2.0 fusion.40
  328.7 0.3 copy.83
  329.2 0.3 copy.84
  329.5 9.0 %multiply_reduce_fusion.1 = (f32[128]{0:T(128)S(1)}, f32[128,3584]{1,0:T(8,128)S(1)}) fusion(f32[3584]{0:T(1024)} %get-tuple-element.23, bf16[3584,1792]{1,0:T(8,128)(2,1)} %bitcast.39, f32[128,1792]{1,0:T(8,128)S(1)} %get-tuple-element.33, f32[128,1792]{1,0:T(8,128)S(1)} %copy.84), kind=kOutput, calls=%fused_computation.19 | convolution fusion | flops 1646919552 | bytes 16529920 | tf_op jit(solution)/shard_map/dot_general | solution.py:242
  338.4 7.5 %fusion.41 = (f32[128,1792]{1,0:T(8,128)S(1)}, f32[128,1792]{1,0:T(8,128)}) fusion(bf16[3584,1792]{1,0:T(8,128)(2,1)} %bitcast.36, f32[128,3584]{1,0:T(8,128)S(1)} %get-tuple-element.35, f32[3584]{0:T(1024)S(1)} %get-tuple-element.22, f32[128]{0:T(128)S(1)} %add_rsqrt_fusion.4), kind=kOutput, calls=%fused_computation.85 | convolution fusion | flops 1646231552 | bytes 16529920 | tf_op jit(solution)/shard_map/dot_general | solution.py:234
  345.9 0.3 copy.85
  346.4 0.3 copy.86
  346.7 0.3 copy-done.2
  346.9 9.3 %multiply_reduce_fusion = (f32[128]{0:T(128)S(1)}, f32[128,3584]{1,0:T(8,128)S(1)}) fusion(f32[3584]{0:T(1024)S(1)} %copy-done.2, bf16[3584,1792]{1,0:T(8,128)(2,1)} %bitcast.38, f32[128,1792]{1,0:T(8,128)} %get-tuple-element.37, f32[128,1792]{1,0:T(8,128)S(1)} %copy.86), kind=kOutput, calls=%fused_computation.17 | convolution fusion | flops 1646919552 | bytes 16529920 | tf_op jit(solution)/shard_map/dot_general | solution.py:242
  356.2 0.9 copy.80
  357.1 0.7 multiply_add_fusion.1
  357.8 4.4 multiply_reduce_fusion.2
  362.3 1.5 convolution_convert_fusion.2
  363.8 4.4 all_to_all.33
  368.1 7.8 %reduce.17 = bf16[256,2048]{1,0:T(8,128)(2,1)} reduce(bf16[256,1,2048]{2,1,0:T(2,128)(2,1)S(1)} %all_to_all.33, bf16[]{:T(256)} %broadcast.123), dimensions={1}, to_apply=%all_to_all.33.reduce_sub_computation | reduce | bytes 2097154 | tf_op jit(solution)/shard_map/all_to_all | solution.py:310
  375.9 2.7 reshape.192
  378.6 13.8 %all-to-all-start.1 = ((bf16[256,2,1024]{2,1,0:T(2,128)(2,1)}), bf16[256,2,1024]{2,1,0:T(2,128)(2,1)}, u32[]{:S(2)}, u32[]{:S(2)}) async-start(bf16[256,2,1024]{2,1,0:T(2,128)(2,1)} %reshape.192), calls=%async_computation.1 | async-start | bytes 2097152 | tf_op jit(solution)/shard_map/all_to_all | solution.py:310
  392.4 0.2 convolution_bitcast_fusion
  392.6 0.3 convolution_convert_fusion.3
  392.9 0.2 reshape.191
  393.2 1.6 reduce
  395.2 28.6 %all-to-all-done.1 = bf16[256,2,1024]{2,1,0:T(2,128)(2,1)} async-done(((bf16[256,2,1024]{2,1,0:T(2,128)(2,1)}), bf16[256,2,1024]{2,1,0:T(2,128)(2,1)}, u32[]{:S(2)}, u32[]{:S(2)}) %all-to-all-start.1) | async-done | bytes 1048608 | tf_op jit(solution)/shard_map/all_to_all | solution.py:310
  423.8 6.4 %reshape.193 = bf16[256,1,2048]{2,1,0:T(2,128)(2,1)S(1)} reshape(bf16[256,2,1024]{2,1,0:T(2,128)(2,1)} %all-to-all-done.1) | data formatting | bytes 2097152
  430.2 7.1 %reduce.6 = bf16[256,2048]{1,0:T(8,128)(2,1)} reduce(bf16[256,1,2048]{2,1,0:T(2,128)(2,1)S(1)} %reshape.193, bf16[]{:T(256)} %constant.38), dimensions={1}, to_apply=%all_to_all.27.reduce_sub_computation | reduce | bytes 2097154 | tf_op jit(solution)/shard_map/all_to_all | solution.py:310
  437.3 1.4 reshape.159
  438.7 0.5 fusion.42
  439.3 0.2 fusion.28
  439.5 0.2 convert_element_type.123
  439.8 0.7 reduce.19
  440.6 0.7 reshape.196
  441.3 5.3 %all-to-all-start.3 = ((bf16[256,2,128]{2,1,0:T(2,128)(2,1)}), bf16[256,2,128]{2,1,0:T(2,128)(2,1)S(1)}, u32[]{:S(2)}, u32[]{:S(2)}) async-start(bf16[256,2,128]{2,1,0:T(2,128)(2,1)} %reshape.196), calls=%async_computation.3 | async-start | bytes 262144 | tf_op jit(solution)/shard_map/all_to_all | solution.py:310
  446.6 0.5 multiply_convert_fusion
  447.1 3.3 all_to_all.34
  450.4 8.0 %reduce.18 = bf16[256,2048]{1,0:T(8,128)(2,1)S(1)} reduce(bf16[256,1,2048]{2,1,0:T(2,128)(2,1)} %all_to_all.34, bf16[]{:T(256)} %broadcast.123), dimensions={1}, to_apply=%all_to_all.34.reduce_sub_computation | reduce | bytes 2097154 | tf_op jit(solution)/shard_map/all_to_all | solution.py:310
  458.4 1.6 reshape.194
  460.0 14.6 %all-to-all-start.2 = ((bf16[256,2,1024]{2,1,0:T(2,128)(2,1)}), bf16[256,2,1024]{2,1,0:T(2,128)(2,1)}, u32[]{:S(2)}, u32[]{:S(2)}) async-start(bf16[256,2,1024]{2,1,0:T(2,128)(2,1)} %reshape.194), calls=%async_computation.2 | async-start | bytes 2097152 | tf_op jit(solution)/shard_map/all_to_all | solution.py:310
  474.7 0.3 convolution_multiply_fusion.2
  475.0 1.7 fusion.35
  476.7 0.8 reduce.8
  477.7 0.2 fusion.18
  477.9 0.2 reshape.163
  478.1 0.6 copy.92
  478.7 27.4 %all-to-all-done.2 = bf16[256,2,1024]{2,1,0:T(2,128)(2,1)} async-done(((bf16[256,2,1024]{2,1,0:T(2,128)(2,1)}), bf16[256,2,1024]{2,1,0:T(2,128)(2,1)}, u32[]{:S(2)}, u32[]{:S(2)}) %all-to-all-start.2) | async-done | bytes 1048608 | tf_op jit(solution)/shard_map/all_to_all | solution.py:310
  506.1 6.4 %reshape.195 = bf16[256,1,2048]{2,1,0:T(2,128)(2,1)S(1)} reshape(bf16[256,2,1024]{2,1,0:T(2,128)(2,1)} %all-to-all-done.2) | data formatting | bytes 2097152
  512.5 7.1 %reduce.7 = bf16[256,2048]{1,0:T(8,128)(2,1)} reduce(bf16[256,1,2048]{2,1,0:T(2,128)(2,1)S(1)} %reshape.195, bf16[]{:T(256)} %constant.38), dimensions={1}, to_apply=%all_to_all.29.reduce_sub_computation | reduce | bytes 2097154 | tf_op jit(solution)/shard_map/all_to_all | solution.py:310
  519.7 1.4 reshape.160
  521.1 1.1 fusion.43
  (50 shorter events, 1.4 us)
Async XLA Ops:
  0.6 391.9 %copy-start = (bf16[256,1024]{1,0:T(8,128)(2,1)S(1)}, bf16[256,1024]{1,0:T(8,128)(2,1)}, u32[]{:S(2)}) copy-start(bf16[256,1024]{1,0:T(8,128)(2,1)} %param.20) | copy-start | bytes 1572868
  1.8 1.3 copy-start.5
  6.9 371.6 %all-to-all-start = ((bf16[256,2,256]{2,1,0:T(2,128)(2,1)}), bf16[256,2,256]{2,1,0:T(2,128)(2,1)S(1)}, u32[]{:S(2)}, u32[]{:S(2)}) async-start(bf16[256,2,256]{2,1,0:T(2,128)(2,1)} %reshape.190), calls=%async_computation | async-start | bytes 524288 | tf_op jit(solution)/shard_map/all_to_all | solution.py:310
  285.8 30.5 %copy-start.3 = (f32[1,3584]{1,0:T(1,128)S(1)}, f32[1,3584]{1,0:T(1,128)}, u32[]{:S(2)}) copy-start(f32[1,3584]{1,0:T(1,128)} %param.14) | copy-start | bytes 43012
  285.8 40.7 %copy-start.1 = (bf16[128,3584]{1,0:T(8,128)(2,1)S(1)}, bf16[128,3584]{1,0:T(8,128)(2,1)}, u32[]{:S(2)}) copy-start(bf16[128,3584]{1,0:T(8,128)(2,1)} %param.12) | copy-start | bytes 2752516
  346.2 0.7 copy-start.2
  357.8 4.4 copy-start.4
  375.9 16.5 %copy-start.7 = (s32[1,128]{1,0:T(1,128)S(1)}, s32[1,128]{1,0:T(1,128)}, u32[]{:S(2)}) copy-start(s32[1,128]{1,0:T(1,128)} %param.22) | copy-start | bytes 1540
  375.9 16.5 %copy-start.8 = (f32[256]{0:T(256)S(1)}, f32[256]{0:T(256)}, u32[]{:S(2)}) copy-start(f32[256]{0:T(256)} %param.21) | copy-start | bytes 3076
  378.6 45.2 %all-to-all-start.1 = ((bf16[256,2,1024]{2,1,0:T(2,128)(2,1)}), bf16[256,2,1024]{2,1,0:T(2,128)(2,1)}, u32[]{:S(2)}, u32[]{:S(2)}) async-start(bf16[256,2,1024]{2,1,0:T(2,128)(2,1)} %reshape.192), calls=%async_computation.1 | async-start | bytes 2097152 | tf_op jit(solution)/shard_map/all_to_all | solution.py:310
  441.3 18.8 %all-to-all-start.3 = ((bf16[256,2,128]{2,1,0:T(2,128)(2,1)}), bf16[256,2,128]{2,1,0:T(2,128)(2,1)S(1)}, u32[]{:S(2)}, u32[]{:S(2)}) async-start(bf16[256,2,128]{2,1,0:T(2,128)(2,1)} %reshape.196), calls=%async_computation.3 | async-start | bytes 262144 | tf_op jit(solution)/shard_map/all_to_all | solution.py:310
  460.0 46.1 %all-to-all-start.2 = ((bf16[256,2,1024]{2,1,0:T(2,128)(2,1)}), bf16[256,2,1024]{2,1,0:T(2,128)(2,1)}, u32[]{:S(2)}, u32[]{:S(2)}) async-start(bf16[256,2,1024]{2,1,0:T(2,128)(2,1)} %reshape.194), calls=%async_computation.2 | async-start | bytes 2097152 | tf_op jit(solution)/shard_map/all_to_all | solution.py:310
  474.7 3.0 copy-start.6

commit v2 on v0

v2 whole, which is shorter than its diff:
```python
import functools

import jax
import jax.numpy as jnp
from jax import lax
from jax.experimental import pallas as pl
from jax.experimental.pallas import tpu as pltpu
from jax.sharding import PartitionSpec as P

HD = 128
MESH = pl.DeviceIdType.MESH
F32 = jnp.float32
BF16 = jnp.bfloat16

eps = 1e-06
temper = 4.0
UNUSED = -1e30

SIZES = (4, 4, 8)
ORDERS = ((0, 1, 2), (2, 1, 0), (0, 2, 1))
PART_ROWS = (32, 48, 32)


def dot(a, b, contract=((1,), (0,))):
    return lax.dot_general(a, b, (contract, ((), ())), preferred_element_type=F32)


def normalize(values, scale_row):
    return values * lax.rsqrt(jnp.mean(values * values, axis=-1, keepdims=True) + eps) * scale_row


def offsets_along(size):
    return [0] + list(range(1, size // 2 + 1)) + [-k for k in range(1, size // 2)]


def gather_plan(latency=25.0):
    rows = {}
    for part, order in enumerate(ORDERS):
        for phase, axis in enumerate(order):
            if phase == 0:
                subs = [()]
            elif phase == 1:
                subs = [(k,) for k in offsets_along(SIZES[order[0]])]
            else:
                subs = [(None, k) for k in offsets_along(SIZES[order[1]])]
            for sub in subs:
                count = PART_ROWS[part] * (SIZES[order[0]] if phase == 2 else 1)
                for k in offsets_along(SIZES[axis]):
                    if k:
                        rows[part, phase, k, sub] = count

    def waits_for(hop):
        part, phase, k, sub = hop
        if abs(k) > 1:
            return [(part, phase, k - 1 if k > 0 else k + 1, sub)]
        if phase == 0:
            return []
        if phase == 1:
            return [(part, 0, sub[0], ())] if sub[0] else []
        found = []
        for j in offsets_along(SIZES[ORDERS[part][0]]):
            if sub[1]:
                found.append((part, 1, sub[1], (j,)))
            elif j:
                found.append((part, 0, j, ()))
        return found

    needs = {hop: waits_for(hop) for hop in rows}
    done, free, todo = {}, {}, set(rows)
    while todo:
        best = None
        for hop in todo:
            if all(d in done for d in needs[hop]):
                ready = max([done[d] for d in needs[hop]], default=0.0)
                axis = ORDERS[hop[0]][hop[1]]
                start = max(ready, free.get(axis, 0.0))
                key = (start, hop[1], ready, -hop[2], str(hop))
                if best is None or key < best[0]:
                    best = (key, hop, axis, start)
        _, hop, axis, start = best
        free[axis] = start + rows[hop]
        done[hop] = free[axis] + latency
        todo.discard(hop)
    return sorted(rows, key=lambda hop: (done[hop], str(hop))), needs


def coordinates(index):
    return (index // 64, index % 64)


def gather_kernel(
    plan,
    needs,
    shard_ref,
    gain_ref,
    side_ref,
    out_ref,
    gains_ref,
    got_side_ref,
    away,
    came,
    block,
    local_sem,
    gain_local,
    side_local,
    pair_send,
    pair_recv,
    gain_send,
    gain_recv,
    side_send,
    side_recv,
    send_sem,
    recv_sem,
    sib_send,
    sib_recv,
):
    x = lax.axis_index("segment")
    dp = lax.axis_index("dp")
    me = x * 64 + dp
    core = dp % 2
    z = (dp // 2) % SIZES[2]
    y = dp // (2 * SIZES[2])
    here = (x, y, z)
    sign = 1 - 2 * core
    owners = side_ref.shape[0]

    barrier = pltpu.get_barrier_semaphore()

    @pl.loop(1, owners)
    def _(i):
        other = (me + i) % owners
        pl.semaphore_signal(barrier, inc=1, device_id=coordinates(other), device_id_type=MESH)

    rows, width = shard_ref.shape
    half = width // 2
    keep = shard_ref[:, pl.ds(pl.multiple_of(core * half, HD), half)].astype(F32)
    other_half = shard_ref[:, pl.ds(pl.multiple_of((1 - core) * half, HD), half)].astype(F32)
    spare = jnp.zeros((away.shape[0] - rows, half), F32)
    away[...] = jnp.concatenate([other_half, spare], axis=0).astype(BF16)
    gain_copy = pltpu.make_async_copy(gain_ref, gains_ref.at[x], gain_local)
    gain_copy.start()
    side_copy = pltpu.make_async_copy(side_ref.at[me], got_side_ref.at[me], side_local)
    side_copy.start()

    pl.semaphore_wait(barrier, owners - 1)

    def device(at, on):
        return (at[0], (at[1] * SIZES[2] + at[2]) * 2 + on)

    def reach(axis, k, way):
        return (here[axis] + way * k + 2 * SIZES[axis]) % SIZES[axis]

    sibling = device(here, 1 - core)
    pair = pltpu.make_async_remote_copy(
        src_ref=away,
        dst_ref=came,
        send_sem=pair_send,
        recv_sem=pair_recv,
        device_id=sibling,
        device_id_type=MESH,
    )
    pair.start()
    gain_copies = []
    for k in range(1, SIZES[0]):
        copy = pltpu.make_async_remote_copy(
            src_ref=gain_ref,
            dst_ref=gains_ref.at[x],
            send_sem=gain_send.at[k - 1],
            recv_sem=gain_recv.at[k - 1],
            device_id=(reach(0, k, 1), dp),
            device_id_type=MESH,
        )
        copy.start()
        gain_copies.append(copy)
    pair.wait_recv()
    theirs = came[...].astype(F32)[:rows]

    @pl.when(core == 0)
    def _():
        block[...] = jnp.concatenate([keep, theirs], axis=0).astype(BF16)

    @pl.when(core == 1)
    def _():
        block[...] = jnp.concatenate([theirs, keep], axis=0).astype(BF16)

    mine = pltpu.make_async_copy(block, out_ref.at[core, x, y, z], local_sem)
    mine.start()
    mine.wait()

    starts = [sum(PART_ROWS[:part]) for part in range(len(PART_ROWS))]
    number = {hop: i for i, hop in enumerate(plan)}

    def held(hop, travelled, on, way):
        part, phase, _, sub = hop
        order = ORDERS[part]
        at = list(here)
        at[order[phase]] = reach(order[phase], -travelled, way)
        for axis, k in zip(order[:phase], sub):
            at[axis] = slice(None) if k is None else reach(axis, -k, way)
        return out_ref.at[
            on, at[0], at[1], at[2], pl.ds(starts[part], PART_ROWS[part]), :
        ]

    def hop_copy(hop, sending):
        part, phase, k, _ = hop
        axis = ORDERS[part][phase]
        step = 1 if k > 0 else -1
        ref = held(hop, k - step if sending else k, core, sign)
        to = list(here)
        to[axis] = reach(axis, step, sign)
        return pltpu.make_async_remote_copy(
            src_ref=ref,
            dst_ref=ref,
            send_sem=send_sem.at[number[hop]],
            recv_sem=recv_sem.at[number[hop]],
            device_id=device(to, core),
            device_id_type=MESH,
        )

    def share(hop, on, way):
        ref = out_ref.at[on, x, y, z] if hop is None else held(hop, hop[2], on, way)
        index = len(plan) if hop is None else number[hop]
        return pltpu.make_async_remote_copy(
            src_ref=ref,
            dst_ref=ref,
            send_sem=sib_send.at[index],
            recv_sem=sib_recv.at[index],
            device_id=sibling,
            device_id_type=MESH,
        )

    sends = []
    started, arrived = set(), set()

    def launch(copy):
        copy.start()
        sends.append(copy)

    def start_ready():
        for hop in plan:
            if hop not in started and all(d in arrived for d in needs[hop]):
                launch(hop_copy(hop, True))
                started.add(hop)

    start_ready()
    launch(share(None, core, sign))

    @pl.loop(1, owners)
    def _(i):
        other = (me + i) % owners
        pltpu.make_async_remote_copy(
            src_ref=side_ref.at[other],
            dst_ref=got_side_ref.at[me],
            send_sem=side_send,
            recv_sem=side_recv,
            device_id=coordinates(other),
            device_id_type=MESH,
        ).start()

    for hop in plan:
        hop_copy(hop, False).wait_recv()
        arrived.add(hop)
        start_ready()
        launch(share(hop, core, sign))

    for hop in [None] + plan:
        share(hop, 1 - core, -sign).wait_recv()
    for copy in sends:
        copy.wait_send()
    pair.wait_send()
    gain_copy.wait()
    side_copy.wait()
    for k, copy in enumerate(gain_copies):
        copy.wait_send()
        behind = gains_ref.at[reach(0, -(k + 1), 1)]
        pltpu.make_async_copy(behind, behind, gain_recv.at[k]).wait()
    most = got_side_ref.at[pl.ds(0, owners - 1)]
    pltpu.make_async_copy(most, most, side_send).wait()
    pltpu.make_async_copy(most, most, side_recv).wait()


def gather_weights(shard, gain, side):
    rows, width = shard.shape
    plan, needs = gather_plan()
    hops = len(plan)
    half = width // 2
    anywhere = pl.BlockSpec(memory_space=pl.ANY)
    dma = pltpu.SemaphoreType.DMA
    return pl.pallas_call(
        functools.partial(gather_kernel, plan, needs),
        out_shape=(
            jax.ShapeDtypeStruct((2, *SIZES, 2 * rows, half), shard.dtype),
            jax.ShapeDtypeStruct((SIZES[0], *gain.shape), gain.dtype),
            jax.ShapeDtypeStruct(side.shape, side.dtype),
        ),
        in_specs=[pl.BlockSpec(memory_space=pltpu.VMEM), anywhere, anywhere],
        out_specs=(anywhere, anywhere, anywhere),
        scratch_shapes=[
            pltpu.VMEM((64, half), BF16),
            pltpu.VMEM((64, half), BF16),
            pltpu.VMEM((2 * rows, half), BF16),
            dma,
            dma,
            dma,
            dma,
            dma,
            dma((SIZES[0] - 1,)),
            dma((SIZES[0] - 1,)),
            dma,
            dma,
            dma((hops,)),
            dma((hops,)),
            dma((hops + 1,)),
            dma((hops + 1,)),
        ],
        compiler_params=pltpu.CompilerParams(
            collective_id=0, has_side_effects=True, vmem_limit_bytes=16 << 20
        ),
        name="gather_weights",
    )(shard, gain, side)


def teacher_kernel(
    steps,
    items_ref,
    gains_ref,
    weight_ref,
    student_gain_ref,
    out_gain_ref,
    adapter_ref,
    out_ref,
    total,
    act,
    adapter,
    adapter_sem,
):
    step = pl.program_id(0)
    section = step // steps
    inner = step % steps
    depth, half = weight_ref.shape[2] * weight_ref.shape[3], weight_ref.shape[4]
    width = 2 * half
    is_value = section % 2 == 0
    begins = inner == 0
    part = inner % 2
    chunk = inner // 2

    @pl.when(step == 0)
    def _():
        pltpu.make_async_copy(adapter_ref, adapter, adapter_sem).start()
        act[...] = normalize(items_ref[...].astype(F32), gains_ref[0]).astype(BF16)

    @pl.when(begins & (step > 0) & is_value)
    def _():
        hidden = (total[...] * gains_ref[section - 1]).astype(BF16).astype(F32)
        act[...] = normalize(hidden, gains_ref[section]).astype(BF16)

    @pl.when(begins & jnp.logical_not(is_value))
    def _():
        for head in range(width // HD):
            cols = slice(head * HD, (head + 1) * HD)
            values = total[:, cols].astype(BF16).astype(F32)
            scale = lax.rsqrt(jnp.mean(values * values, axis=-1, keepdims=True) + eps)
            act[:, cols] = (values * scale).astype(BF16)

    @pl.when(begins)
    def _():
        total[...] = jnp.zeros_like(total)

    weight = weight_ref[0, 0].reshape(depth, half)

    @pl.when(is_value)
    def _():
        lhs = act[:, pl.ds(pl.multiple_of(chunk * depth, HD), depth)]
        cols = pl.ds(pl.multiple_of(part * half, HD), half)
        total[:, cols] += dot(lhs, weight)

    @pl.when(jnp.logical_not(is_value))
    def _():
        lhs = act[:, pl.ds(pl.multiple_of(part * half, HD), half)]
        cols = pl.ds(pl.multiple_of(chunk * depth, HD), depth)
        total[:, cols] += dot(lhs, weight, ((1,), (1,)))

    @pl.when(step == pl.num_programs(0) - 1)
    def _():
        outcome = (total[...] * gains_ref[section]).astype(BF16).astype(F32)
        act[...] = normalize(outcome, student_gain_ref[...]).astype(BF16)
        pltpu.make_async_copy(adapter_ref, adapter, adapter_sem).wait()
        raw = dot(act[...], adapter[...])
        out_ref[...] = normalize(raw, out_gain_ref[...]).astype(BF16)


def teacher(items, gains, gathered, student_gain, adapter, out_gain):
    rows, width = items.shape
    sections = gathered.shape[1]
    weights = gathered.reshape(2, sections, -1, *gathered.shape[-2:])
    blocks = 8
    steps = 2 * weights.shape[2] // blocks
    whole = lambda *shape: pl.BlockSpec(shape, lambda step: (0,) * len(shape))
    return pl.pallas_call(
        functools.partial(teacher_kernel, steps),
        out_shape=jax.ShapeDtypeStruct((rows, adapter.shape[1]), BF16),
        grid=(sections * steps,),
        in_specs=[
            whole(rows, width),
            whole(sections, 1, width),
            pl.BlockSpec(
                (1, 1, blocks, *weights.shape[-2:]),
                lambda step: (step % 2, step // steps, step % steps // 2, 0, 0),
            ),
            whole(1, width),
            whole(1, adapter.shape[1]),
            pl.BlockSpec(memory_space=pl.ANY),
        ],
        out_specs=whole(rows, adapter.shape[1]),
        scratch_shapes=[
            pltpu.VMEM((rows, width), F32),
            pltpu.VMEM((rows, width), BF16),
            pltpu.VMEM(adapter.shape, BF16),
            pltpu.SemaphoreType.DMA,
        ],
        compiler_params=pltpu.CompilerParams(vmem_limit_bytes=40 << 20),
        name="teacher_chain",
    )(items, gains, weights, student_gain.reshape(1, -1), out_gain.reshape(1, -1), adapter)


def log_softmax(values):
    shifted = values - jnp.max(values, axis=-1, keepdims=True)
    return shifted - jnp.log(jnp.sum(jnp.exp(shifted), axis=-1, keepdims=True))


def pairs_kernel(
    target_ref,
    embed_ref,
    side_ref,
    bank_ref,
    bias_ref,
    neg_ref,
    emb_grad_ref,
    bank_grad_ref,
    kl_ref,
    out_buf,
    got,
    home,
    kl_out,
    kl_home,
    wide,
    slots,
    negatives,
    local_sems,
    send_sem,
    recv_sem,
    back_send,
    back_recv,
    kl_send,
    kl_recv,
):
    me = lax.axis_index("segment") * 64 + lax.axis_index("dp")
    owners, lines, lanes = got.shape
    rows, embed_width = embed_ref.shape
    splits = embed_width // lanes
    picks = target_ref.shape[0]
    capacity = lines // splits
    score_scale = temper * embed_width ** (-0.5)

    barrier = pltpu.get_barrier_semaphore()

    @pl.loop(1, owners)
    def _(i):
        other = (me + i) % owners
        pl.semaphore_signal(barrier, inc=1, device_id=coordinates(other), device_id_type=MESH)

    def send_map(rank):
        slot = lax.broadcasted_iota(jnp.int32, (owners, rows), 0) * capacity + rank
        hit = target_ref[0:1, :] == slot
        for pick in range(1, picks):
            hit = hit | (target_ref[pick : pick + 1, :] == slot)
        return hit.astype(F32).astype(BF16)

    def line(rank, split):
        return pl.ds(rank * splits + split, owners, stride=lines)

    for rank in range(capacity):
        sent = dot(send_map(rank), embed_ref[...])
        for split in range(splits):
            wide[line(rank, split), :] = sent[:, split * lanes : (split + 1) * lanes]
    out_buf[...] = wide[...].reshape(owners, lines, lanes).astype(BF16)

    pl.semaphore_wait(barrier, owners - 1)

    def exchange(src, dst, local, send, recv):
        own = pltpu.make_async_copy(src.at[me], dst.at[me], local)
        own.start()

        @pl.loop(1, owners)
        def _(i):
            other = (me + i) % owners
            pltpu.make_async_remote_copy(
                src_ref=src.at[other],
                dst_ref=dst.at[me],
                send_sem=send,
                recv_sem=recv,
                device_id=coordinates(other),
                device_id_type=MESH,
            ).start()

        return own

    def finish(dst, own, send, recv):
        own.wait()
        most = dst.at[pl.ds(0, owners - 1)]
        pltpu.make_async_copy(most, most, recv).wait()
        pltpu.make_async_copy(most, most, send).wait()

    own = exchange(out_buf, got, local_sems.at[0], send_sem, recv_sem)

    pool = bank_ref.shape[0]
    negs = neg_ref.shape[1]
    chosen = neg_ref[...] == lax.broadcasted_iota(jnp.int32, (pool, negs), 0)
    choose = chosen.astype(F32).astype(BF16)
    negatives[...] = dot(choose, bank_ref[...], ((0,), (0,))).astype(BF16)
    offsets = jnp.sum(jnp.where(chosen, bias_ref[...], 0.0), axis=0, keepdims=True)
    valid = (side_ref[:, 0:1] > 0.5 * UNUSED).astype(F32)
    teacher_log = log_softmax(side_ref[...])
    teacher_prob = jnp.exp(teacher_log)

    finish(got, own, send_sem, recv_sem)
    wide[...] = got[...].astype(F32).reshape(owners * lines, lanes)
    for rank in range(capacity):
        for split in range(splits):
            slots[rank * owners : (rank + 1) * owners, split * lanes : (split + 1) * lanes] = wide[
                line(rank, split), :
            ].astype(BF16)

    logits = dot(slots[...], negatives[...], ((1,), (1,))) * score_scale + offsets
    student_log = log_softmax(logits)
    divergence = jnp.sum(teacher_prob * (teacher_log - student_log), axis=-1, keepdims=True)
    divergence = divergence.astype(BF16).astype(F32)
    lane = lax.broadcasted_iota(jnp.int32, (owners, lanes), 1)
    spread = jnp.zeros((owners, lanes), F32)
    for rank in range(capacity):
        spread = jnp.where(lane == rank, divergence[rank * owners : (rank + 1) * owners], spread)
    kl_out[...] = spread.reshape(owners, 1, lanes)
    kl_own = exchange(kl_out, kl_home, local_sems.at[1], kl_send, kl_recv)

    gap = (valid * (jnp.exp(student_log) - teacher_prob)).astype(BF16)
    for rank in range(capacity):
        grad = dot(gap[rank * owners : (rank + 1) * owners], negatives[...]) * score_scale
        for split in range(splits):
            wide[line(rank, split), :] = grad[:, split * lanes : (split + 1) * lanes]
    out_buf[...] = wide[...].reshape(owners, lines, lanes).astype(BF16)
    own = exchange(out_buf, home, local_sems.at[2], back_send, back_recv)

    rest = dot(gap, slots[...], ((0,), (0,))) * score_scale
    bank_grad = jnp.zeros(bank_grad_ref.shape, F32)
    for _ in range(3):
        term = rest.astype(BF16)
        bank_grad = bank_grad + dot(choose, term)
        rest = rest - term.astype(F32)
    bank_grad_ref[...] = bank_grad

    finish(kl_home, kl_own, kl_send, kl_recv)
    kl_ref[...] = kl_home[...].reshape(owners, lanes)
    finish(home, own, back_send, back_recv)
    wide[...] = home[...].astype(F32).reshape(owners * lines, lanes)
    for rank in range(capacity):
        for split in range(splits):
            slots[rank * owners : (rank + 1) * owners, split * lanes : (split + 1) * lanes] = wide[
                line(rank, split), :
            ].astype(BF16)
    emb_grad = jnp.zeros(emb_grad_ref.shape, F32)
    for rank in range(capacity):
        held = slots[rank * owners : (rank + 1) * owners, :]
        emb_grad = emb_grad + dot(send_map(rank), held, ((0,), (0,)))
    emb_grad_ref[...] = emb_grad


def pairs(target, embedding, side, bank, bank_bias, neg_index, owners, capacity):
    rows, embed_width = embedding.shape
    lines = capacity * embed_width // HD
    vmem = pl.BlockSpec(memory_space=pltpu.VMEM)
    dma = pltpu.SemaphoreType.DMA
    return pl.pallas_call(
        pairs_kernel,
        out_shape=(
            jax.ShapeDtypeStruct((rows, embed_width), F32),
            jax.ShapeDtypeStruct(bank.shape, F32),
            jax.ShapeDtypeStruct((owners, HD), F32),
        ),
        in_specs=[vmem] * 6,
        out_specs=(vmem,) * 3,
        scratch_shapes=[
            pltpu.VMEM((owners, lines, HD), BF16),
            pltpu.VMEM((owners, lines, HD), BF16),
            pltpu.VMEM((owners, lines, HD), BF16),
            pltpu.VMEM((owners, 1, HD), F32),
            pltpu.VMEM((owners, 1, HD), F32),
            pltpu.VMEM((owners * lines, HD), F32),
            pltpu.VMEM((owners * capacity, embed_width), BF16),
            pltpu.VMEM((neg_index.shape[1], embed_width), BF16),
            dma((3,)),
            dma,
            dma,
            dma,
            dma,
            dma,
            dma,
        ],
        compiler_params=pltpu.CompilerParams(
            collective_id=1, has_side_effects=True, vmem_limit_bytes=40 << 20
        ),
        name="pair_exchange",
    )(target, embedding, side, bank, bank_bias.reshape(-1, 1), neg_index)


def shards(
    items,
    section_weights,
    section_gains,
    student_gain,
    adapter,
    out_gain,
    assign,
    teacher_scores,
    bank,
    bank_bias,
    neg_index,
):
    owners = lax.axis_size("segment") * lax.axis_size("dp")
    row_count, pick_count = assign.shape
    pair_count = row_count * pick_count
    capacity = 2
    slot_count = owners * capacity

    pair_cluster = assign.reshape(-1)
    same = pair_cluster[:, None] == pair_cluster[None, :]
    earlier = jnp.arange(pair_count)[:, None] > jnp.arange(pair_count)[None, :]
    pair_rank = jnp.sum((same & earlier).astype(jnp.int32), axis=1)
    target = pair_cluster * capacity + pair_rank
    pick_map = target[None, :] == jnp.arange(slot_count, dtype=jnp.int32)[:, None]
    scores = teacher_scores.reshape(pair_count, -1)
    side = jnp.dot(pick_map.astype(BF16), scores, preferred_element_type=F32)
    side = jnp.where(jnp.any(pick_map, axis=1, keepdims=True), side, UNUSED)
    side = side.reshape(owners, capacity, -1)

    gathered, gains, got_side = gather_weights(
        section_weights[0], section_gains.reshape(1, -1), side
    )
    embedding = teacher(items, gains, gathered, student_gain, adapter, out_gain)
    slot_side = got_side.transpose(1, 0, 2).reshape(slot_count, -1)
    target_rows = target.reshape(row_count, pick_count).T
    emb_grad, bank_grad, owner_kl = pairs(
        target_rows, embedding, slot_side, bank, bank_bias, neg_index, owners, capacity
    )
    slot_kl = owner_kl[:, :capacity].reshape(slot_count)
    row_kl = jnp.sum(jnp.where(pick_map, slot_kl[:, None], 0.0), axis=0)
    row_kl = row_kl.astype(BF16).reshape(row_count, pick_count)
    return (emb_grad, row_kl, bank_grad)


def solution(mesh):
    in_specs = (
        P(("segment", "dp"), None),
        P("segment", "dp", None),
        P("segment", None),
        P(),
        P(),
        P(),
        P(("segment", "dp"), None),
        P(("segment", "dp"), None, None),
        P(("segment", "dp"), None),
        P(("segment", "dp")),
        P(("segment", "dp"), None),
    )
    out_specs = (P(("segment", "dp"), None), P(("segment", "dp"), None), P(("segment", "dp"), None))
    return jax.shard_map(shards, mesh=mesh, in_specs=in_specs, out_specs=out_specs, check_vma=False)
```

time: 565 us -> 271 us (0.48); the launches traced: 557 us -> 270 us
  waiting for transfers between devices: 353 us -> 0 us
  Pallas kernels: 0 us -> 257 us
  starting transfers between devices: 72.4 us -> 0 us
  matrix products: 36.6 us -> 0.24 us
  local copies, waits for them, and re-layouts: 45.8 us -> 11.3 us
  loops' own time: 31.8 us -> 0 us
  between operations: 15.3 us -> 0.76 us
    pallas_call x0 -> x3, Pallas kernels: none -> 257 us  [the longest x1 146 us: gather_weights(): pl.pallas_call(functools.partial(gather_kernel, plan, needs), out_shape=(...]
    ppermute x8 -> x0, waiting for transfers between devices: 145 us -> none  [from_behind(): return lax.ppermute(block, axis, route)]
    all_to_all x10 -> x0, waiting for transfers between devices: 112 us -> none  [the longest x1 27 us: shards(): lax.all_to_all(lax.all_to_all(sent_embed, 'segment', split_axis=0, concat...]
    all_gather x1 -> x0, waiting for transfers between devices: 95.9 us -> none  [shards(): weight = lax.all_gather(section_weights[0], 'dp', axis=0, tiled=True)]
    all_to_all x10 -> x0, starting transfers between devices: 55.9 us -> none  [the longest x1 12.5 us: shards(): lax.all_to_all(lax.all_to_all(sent_valid, 'segment', split_axis=0, concat...]
    dot_general x14 -> x1, matrix products: 36.6 us -> 0.24 us  [shards(): side = jnp.dot(pick_map.astype(BF16), scores, preferred_element_type=F32)]
    another operation x12 -> x0, loops' own time: 31.8 us -> none  [the longest x8 31.2 us: run_ticks(): carried = lax.cond(is_due, apply_section, lambda held: held, carried)]
    ppermute x8 -> x0, starting transfers between devices: 16.4 us -> none  [from_behind(): return lax.ppermute(block, axis, route)]
  transfers between devices with their start and end apart: 19 -> 0, of which waited for: 18 -> 0; matrix products, arithmetic and copies ran while one was open for 4% -> 0% of each run, Pallas kernels for 0% -> 0%
where the time goes in v2:
time: 271 us; the launch traced here: 270 us
  Pallas kernels  257 us (95%)
  local copies, waits for them, and re-layouts  11.3 us (4%)
    pallas_call x1, Pallas kernels, gather_weights(): pl.pallas_call(functools.partial(gather_kernel, plan, needs), out_shape=(...  146 us
    pallas_call x1, Pallas kernels, pairs(): pl.pallas_call(pairs_kernel, out_shape=(jax.ShapeDtypeStruct((rows, embed...  71.5 us
    pallas_call x1, Pallas kernels, teacher(): pl.pallas_call(functools.partial(teacher_kernel, steps), out_shape=jax.Sh...  39.6 us
    unnamed x24, local copies, waits for them, and re-layouts  9.83 us

profile of v2, /device:TPU:1, one launch (start us, length us, event | category | flops | bytes accessed | tf_op | source)
XLA Modules:
  0.0 270.3 jit_solution(9267412479047453570)
XLA Ops:
  0.6 0.0 copy-start
  0.6 0.0 copy-start.3
  0.7 0.8 copy.20
  1.5 0.1 eq.28
  1.6 0.2 convert_reduce_fusion
  1.8 0.2 fusion
  2.0 0.0 copy-done
  2.0 0.2 convolution_select_fusion
  2.3 0.0 copy-start.4
  2.3 0.9 copy-done.4
  3.2 0.0 copy-start.5
  3.2 0.7 copy-done.5
  3.9 0.0 copy-start.8
  3.9 0.0 copy-start.9
  3.9 0.0 copy-start.7
  3.9 146.3 %gather_weights.1 = (bf16[2,4,4,8,112,896]{5,4,3,2,1,0:T(8,128)(2,1)}, f32[4,1,3584]{2,1,0:T(1,128)S(1)}, f32[256,2,128]{2,1,0:T(2,128)S(1)}) custom-call(bf16[56,1792]{1,0:T(8,128)(2,1)S(1)} %bitcast.16, f32[1,3584]{1,0:T(1,128)S(1)} %copy-done.5, f32[256,2,128]{2,1,0:T(2,128)S(1)} %bitcast.15), custom_call_target="tpu_custom_call" | custom-call | tf_op jit(solution)/shard_map/gather_weights/pallas_call | solution.py:289
  150.3 0.7 reshape.48.student_gain_ref
  151.0 0.0 copy-start.1
  151.0 3.1 %copy-done.1 = bf16[3584,1024]{1,0:T(8,128)(2,1)S(1)} copy-done((bf16[3584,1024]{1,0:T(8,128)(2,1)S(1)}, bf16[3584,1024]{1,0:T(8,128)(2,1)}, u32[]{:S(2)}) %copy-start.1) | copy-done | bytes 7340056
  154.1 0.0 copy-start.2
  154.1 1.2 copy-done.2
  155.3 0.0 copy-start.6
  155.3 0.7 copy-done.6
  155.9 39.6 %teacher_chain.1.embed_ref = bf16[128,1024]{1,0:T(8,128)(2,1)S(1)} custom-call(bf16[128,3584]{1,0:T(8,128)(2,1)S(1)} %copy-done.2, f32[4,1,3584]{2,1,0:T(1,128)S(1)} %get-tuple-element.9.gains_ref, bf16[2,4,32,112,896]{4,3,2,1,0:T(8,128)(2,1)} %bitcast.19, f32[1,3584]{1,0:T(1,128)S(1)} %reshape.48.student_gain_ref, f32[1,1024]{1,0:T(1,128)S(1)} %bitcast.18, ...), custom_call_target="tpu_custom_call" | custom-call | tf_op jit(solution)/shard_map/teacher_chain/pallas_call | solution.py:399
  195.6 0.1 reduce_sum.21
  195.7 0.1 copy.21
  195.8 0.0 copy-done.8
  195.8 0.0 copy-done.9
  195.8 0.1 copy.23.bias_ref
  195.9 0.0 copy-done.3
  195.9 0.0 copy-done.7
  195.9 71.5 %pair_exchange.1 = (f32[128,1024]{1,0:T(8,128)S(1)}, f32[256,1024]{1,0:T(8,128)S(1)}, f32[256,128]{1,0:T(8,128)S(1)}) custom-call(s32[2,128]{1,0:T(2,128)S(1)} %add_bitcast_fusion.target_ref, bf16[128,1024]{1,0:T(8,128)(2,1)S(1)} %teacher_chain.1.embed_ref, f32[512,128]{1,0:T(8,128)S(1)} %bitcast.13, bf16[256,1024]{1,0:T(8,128)(2,1)S(1)} %copy-done.3, ...), custom_call_target="tpu_custom_call" | custom-call | tf_op jit(solution)/shard_map/pair_exchange/pallas_call | solution.py:582
  267.4 0.1 broadcast_in_dim.33
  267.6 0.2 select_reduce_fusion
  267.7 0.2 convert_element_type.13
  267.9 0.6 copy.24
  268.5 0.8 copy.27
  269.3 1.0 copy.28
  (3 shorter events, 0.0 us)
Async XLA Ops:
  0.6 1.4 copy-start
  0.6 195.3 %copy-start.3 = (bf16[256,1024]{1,0:T(8,128)(2,1)S(1)}, bf16[256,1024]{1,0:T(8,128)(2,1)}, u32[]{:S(2)}) copy-start(bf16[256,1024]{1,0:T(8,128)(2,1)} %bank_ref.1) | copy-start | bytes 1572868
  2.3 0.9 copy-start.4
  3.2 0.7 copy-start.5
  3.9 191.9 %copy-start.8 = (s32[128,2]{0,1:T(2,128)S(1)}, s32[128,2]{0,1:T(2,128)}, u32[]{:S(2)}) copy-start(s32[128,2]{0,1:T(2,128)} %param.17) | copy-start | bytes 3076
  3.9 191.9 %copy-start.9 = (f32[256]{0:T(256)S(1)}, f32[256]{0:T(256)}, u32[]{:S(2)}) copy-start(f32[256]{0:T(256)} %param.20) | copy-start | bytes 3076
  3.9 192.0 %copy-start.7 = (s32[1,128]{1,0:T(1,128)S(1)}, s32[1,128]{1,0:T(1,128)}, u32[]{:S(2)}) copy-start(s32[1,128]{1,0:T(1,128)} %neg_ref.1) | copy-start | bytes 1540
  151.0 3.1 %copy-start.1 = (bf16[3584,1024]{1,0:T(8,128)(2,1)S(1)}, bf16[3584,1024]{1,0:T(8,128)(2,1)}, u32[]{:S(2)}) copy-start(bf16[3584,1024]{1,0:T(8,128)(2,1)} %adapter_ref.1) | copy-start | bytes 22020100
  154.1 1.2 copy-start.2
  155.3 0.7 copy-start.6

commit v3 on v2

--- a/solution.py
+++ b/solution.py
@@ -19,6 +19,7 @@
 SIZES = (4, 4, 8)
 ORDERS = ((0, 1, 2), (2, 1, 0), (0, 2, 1))
 PART_ROWS = (32, 48, 32)
+GROUPED = (True, False, False)
 
 
 def dot(a, b, contract=((1,), (0,))):
@@ -33,8 +34,8 @@
     return [0] + list(range(1, size // 2 + 1)) + [-k for k in range(1, size // 2)]
 
 
-def gather_plan(latency=25.0):
-    rows = {}
+def gather_plan(window=8, latency=140.0, release=60.0):
+    rows, needs = {}, {}
     for part, order in enumerate(ORDERS):
         for phase, axis in enumerate(order):
             if phase == 0:
@@ -42,9 +43,10 @@
             elif phase == 1:
                 subs = [(k,) for k in offsets_along(SIZES[order[0]])]
             else:
-                subs = [(None, k) for k in offsets_along(SIZES[order[1]])]
+                firsts = [None] if GROUPED[part] else offsets_along(SIZES[order[0]])
+                subs = [(j, k) for j in firsts for k in offsets_along(SIZES[order[1]])]
             for sub in subs:
-                count = PART_ROWS[part] * (SIZES[order[0]] if phase == 2 else 1)
+                count = PART_ROWS[part] * (SIZES[order[0]] if None in sub else 1)
                 for k in offsets_along(SIZES[axis]):
                     if k:
                         rows[part, phase, k, sub] = count
@@ -58,30 +60,76 @@
         if phase == 1:
             return [(part, 0, sub[0], ())] if sub[0] else []
         found = []
-        for j in offsets_along(SIZES[ORDERS[part][0]]):
+        for j in offsets_along(SIZES[ORDERS[part][0]]) if sub[0] is None else [sub[0]]:
             if sub[1]:
                 found.append((part, 1, sub[1], (j,)))
             elif j:
                 found.append((part, 0, j, ()))
         return found
 
-    needs = {hop: waits_for(hop) for hop in rows}
-    done, free, todo = {}, {}, set(rows)
-    while todo:
-        best = None
-        for hop in todo:
-            if all(d in done for d in needs[hop]):
-                ready = max([done[d] for d in needs[hop]], default=0.0)
-                axis = ORDERS[hop[0]][hop[1]]
-                start = max(ready, free.get(axis, 0.0))
-                key = (start, hop[1], ready, -hop[2], str(hop))
-                if best is None or key < best[0]:
-                    best = (key, hop, axis, start)
-        _, hop, axis, start = best
-        free[axis] = start + rows[hop]
-        done[hop] = free[axis] + latency
-        todo.discard(hop)
-    return sorted(rows, key=lambda hop: (done[hop], str(hop))), needs
+    for hop in rows:
+        needs[hop] = waits_for(hop)
+
+    def axis_of(hop):
+        return ORDERS[hop[0]][hop[1]]
+
+    def lane_of(hop):
+        return (axis_of(hop), hop[2] > 0)
+
+    def urgency(hop):
+        size = SIZES[axis_of(hop)]
+        rest = size // 2 - hop[2] if hop[2] > 0 else size // 2 - 1 + hop[2]
+        return (hop[1], -rest, str(hop))
+
+    queues = {(axis, long_way): [] for axis in range(3) for long_way in (True, False)}
+    flying = dict.fromkeys(queues, 0)
+    for hop in rows:
+        if not needs[hop]:
+            queues[lane_of(hop)].append(hop)
+    events, active, landing, leaving, came = [], {}, {}, {}, set()
+    now = 0.0
+    while True:
+        for lane, queue in queues.items():
+            while queue and flying[lane] < window:
+                queue.sort(key=urgency)
+                hop = queue.pop(0)
+                active[hop] = float(rows[hop])
+                flying[lane] += 1
+                events.append((round(now, 3), 2, str(hop), "start", hop))
+        if not (active or landing or leaving):
+            break
+        load = [0, 0, 0]
+        for hop in active:
+            load[axis_of(hop)] += 1
+        step = min(
+            [left * load[axis_of(hop)] for hop, left in active.items()]
+            + [end - now for end in landing.values()]
+            + [end - now for end in leaving.values()]
+        )
+        now += step
+        for hop in list(active):
+            active[hop] -= step / load[axis_of(hop)]
+            if active[hop] < 1e-6:
+                del active[hop]
+                landing[hop] = now + latency
+                leaving[hop] = now + release
+        for hop in [h for h, end in leaving.items() if end <= now + 1e-6]:
+            del leaving[hop]
+            flying[lane_of(hop)] -= 1
+            events.append((round(now, 3), 1, str(hop), "sent", hop))
+        for hop in [h for h, end in landing.items() if end <= now + 1e-6]:
+            del landing[hop]
+            came.add(hop)
+            events.append((round(now, 3), 0, str(hop), "came", hop))
+            for user in rows:
+                if hop in needs[user] and all(d in came for d in needs[user]):
+                    queues[lane_of(user)].append(user)
+    begun = {(lane_of(hop), at) for at, _, _, kind, hop in events if kind == "start"}
+    return [
+        (kind, hop)
+        for at, _, _, kind, hop in sorted(events, key=lambda event: event[:3])
+        if kind != "sent" or (lane_of(hop), at) in begun
+    ]
 
 
 def coordinates(index):
@@ -89,8 +137,7 @@
 
 
 def gather_kernel(
-    plan,
-    needs,
+    events,
     shard_ref,
     gain_ref,
     side_ref,
@@ -188,6 +235,7 @@
     mine.wait()
 
     starts = [sum(PART_ROWS[:part]) for part in range(len(PART_ROWS))]
+    plan = [hop for kind, hop in events if kind == "came"]
     number = {hop: i for i, hop in enumerate(plan)}
 
     def held(hop, travelled, on, way):
@@ -229,43 +277,39 @@
             device_id_type=MESH,
         )
 
-    sends = []
-    started, arrived = set(), set()
-
-    def launch(copy):
-        copy.start()
-        sends.append(copy)
-
-    def start_ready():
-        for hop in plan:
-            if hop not in started and all(d in arrived for d in needs[hop]):
-                launch(hop_copy(hop, True))
-                started.add(hop)
-
-    start_ready()
-    launch(share(None, core, sign))
-
-    @pl.loop(1, owners)
-    def _(i):
-        other = (me + i) % owners
-        pltpu.make_async_remote_copy(
-            src_ref=side_ref.at[other],
-            dst_ref=got_side_ref.at[me],
-            send_sem=side_send,
-            recv_sem=side_recv,
-            device_id=coordinates(other),
-            device_id_type=MESH,
-        ).start()
-
-    for hop in plan:
-        hop_copy(hop, False).wait_recv()
-        arrived.add(hop)
-        start_ready()
-        launch(share(hop, core, sign))
+    def send_side(begin, end):
+        @pl.loop(begin, end)
+        def _(i):
+            other = (me + i) % owners
+            pltpu.make_async_remote_copy(
+                src_ref=side_ref.at[other],
+                dst_ref=got_side_ref.at[me],
+                send_sem=side_send,
+                recv_sem=side_recv,
+                device_id=coordinates(other),
+                device_id_type=MESH,
+            ).start()
+
+    shares = [share(None, core, sign)]
+    shares[0].start()
+    copies = {}
+    pieces = [(begin, min(begin + 32, owners)) for begin in range(1, owners, 32)]
+    for kind, hop in events:
+        if kind == "start":
+            copies[hop] = hop_copy(hop, True)
+            copies[hop].start()
+        elif kind == "sent":
+            copies.pop(hop).wait_send()
+        else:
+            hop_copy(hop, False).wait_recv()
+            if len(shares) > 60 and len(shares) % 16 == 0 and pieces:
+                send_side(*pieces.pop(0))
+            shares.append(share(hop, core, sign))
+            shares[-1].start()
 
     for hop in [None] + plan:
         share(hop, 1 - core, -sign).wait_recv()
-    for copy in sends:
+    for copy in shares + list(copies.values()):
         copy.wait_send()
     pair.wait_send()
     gain_copy.wait()
@@ -281,13 +325,13 @@
 
 def gather_weights(shard, gain, side):
     rows, width = shard.shape
-    plan, needs = gather_plan()
-    hops = len(plan)
+    events = gather_plan()
+    hops = sum(kind == "came" for kind, _ in events)
     half = width // 2
     anywhere = pl.BlockSpec(memory_space=pl.ANY)
     dma = pltpu.SemaphoreType.DMA
     return pl.pallas_call(
-        functools.partial(gather_kernel, plan, needs),
+        functools.partial(gather_kernel, events),
         out_shape=(
             jax.ShapeDtypeStruct((2, *SIZES, 2 * rows, half), shard.dtype),
             jax.ShapeDtypeStruct((SIZES[0], *gain.shape), gain.dtype),
@@ -324,7 +368,8 @@
     steps,
     items_ref,
     gains_ref,
-    weight_ref,
+    left_ref,
+    right_ref,
     student_gain_ref,
     out_gain_ref,
     adapter_ref,
@@ -336,13 +381,12 @@
 ):
     step = pl.program_id(0)
     section = step // steps
-    inner = step % steps
-    depth, half = weight_ref.shape[2] * weight_ref.shape[3], weight_ref.shape[4]
+    chunk = step % steps
+    depth, half = left_ref.shape[2] * left_ref.shape[3], left_ref.shape[4]
     width = 2 * half
     is_value = section % 2 == 0
-    begins = inner == 0
-    part = inner % 2
-    chunk = inner // 2
+    is_output = section % 2 == 1
+    begins = chunk == 0
 
     @pl.when(step == 0)
     def _():
@@ -354,7 +398,7 @@
         hidden = (total[...] * gains_ref[section - 1]).astype(BF16).astype(F32)
         act[...] = normalize(hidden, gains_ref[section]).astype(BF16)
 
-    @pl.when(begins & jnp.logical_not(is_value))
+    @pl.when(begins & is_output)
     def _():
         for head in range(width // HD):
             cols = slice(head * HD, (head + 1) * HD)
@@ -362,23 +406,25 @@
             scale = lax.rsqrt(jnp.mean(values * values, axis=-1, keepdims=True) + eps)
             act[:, cols] = (values * scale).astype(BF16)
 
-    @pl.when(begins)
-    def _():
-        total[...] = jnp.zeros_like(total)
-
-    weight = weight_ref[0, 0].reshape(depth, half)
-
-    @pl.when(is_value)
-    def _():
-        lhs = act[:, pl.ds(pl.multiple_of(chunk * depth, HD), depth)]
-        cols = pl.ds(pl.multiple_of(part * half, HD), half)
-        total[:, cols] += dot(lhs, weight)
-
-    @pl.when(jnp.logical_not(is_value))
-    def _():
-        lhs = act[:, pl.ds(pl.multiple_of(part * half, HD), half)]
-        cols = pl.ds(pl.multiple_of(chunk * depth, HD), depth)
-        total[:, cols] += dot(lhs, weight, ((1,), (1,)))
+    left = left_ref[0, 0].reshape(depth, half)
+    right = right_ref[0, 0].reshape(depth, half)
+    place = pl.ds(pl.multiple_of(chunk * depth, HD), depth)
+
+    @pl.when(begins & is_value)
+    def _():
+        total[:, :half] = dot(act[:, :depth], left)
+        total[:, half:width] = dot(act[:, :depth], right)
+
+    @pl.when((chunk > 0) & is_value)
+    def _():
+        total[:, :half] += dot(act[:, place], left)
+        total[:, half:width] += dot(act[:, place], right)
+
+    @pl.when(is_output)
+    def _():
+        total[:, place] = dot(act[:, :half], left, ((1,), (1,))) + dot(
+            act[:, half:width], right, ((1,), (1,))
+        )
 
     @pl.when(step == pl.num_programs(0) - 1)
     def _():
@@ -393,9 +439,16 @@
     rows, width = items.shape
     sections = gathered.shape[1]
     weights = gathered.reshape(2, sections, -1, *gathered.shape[-2:])
-    blocks = 8
-    steps = 2 * weights.shape[2] // blocks
+    blocks = 16
+    steps = weights.shape[2] // blocks
     whole = lambda *shape: pl.BlockSpec(shape, lambda step: (0,) * len(shape))
+
+    def half(part):
+        return pl.BlockSpec(
+            (1, 1, blocks, *weights.shape[-2:]),
+            lambda step: (part, step // steps, step % steps, 0, 0),
+        )
+
     return pl.pallas_call(
         functools.partial(teacher_kernel, steps),
         out_shape=jax.ShapeDtypeStruct((rows, adapter.shape[1]), BF16),
@@ -403,10 +456,8 @@
         in_specs=[
             whole(rows, width),
             whole(sections, 1, width),
-            pl.BlockSpec(
-                (1, 1, blocks, *weights.shape[-2:]),
-                lambda step: (step % 2, step // steps, step % steps // 2, 0, 0),
-            ),
+            half(0),
+            half(1),
             whole(1, width),
             whole(1, adapter.shape[1]),
             pl.BlockSpec(memory_space=pl.ANY),
@@ -418,9 +469,9 @@
             pltpu.VMEM(adapter.shape, BF16),
             pltpu.SemaphoreType.DMA,
         ],
-        compiler_params=pltpu.CompilerParams(vmem_limit_bytes=40 << 20),
+        compiler_params=pltpu.CompilerParams(vmem_limit_bytes=59 << 20),
         name="teacher_chain",
-    )(items, gains, weights, student_gain.reshape(1, -1), out_gain.reshape(1, -1), adapter)
+    )(items, gains, weights, weights, student_gain.reshape(1, -1), out_gain.reshape(1, -1), adapter)
 
 
 def log_softmax(values):

time: 271 us -> 246 us (0.908)
  Pallas kernels: 257 us -> 235 us
  local copies, waits for them, and re-layouts: 11.3 us -> 8.53 us
    pallas_call x1, Pallas kernels: 39.6 us -> 28.5 us  [teacher(): pl.pallas_call(functools.partial(teacher_kernel, steps), out_shape=jax.Sh...]
    pallas_call x1, Pallas kernels: 146 us -> 137 us  [gather_weights(): pl.pallas_call(functools.partial(gather_kernel, events), out_shape=(jax.S...]
    unnamed x24 -> x22, local copies, waits for them, and re-layouts: 9.83 us -> 6.42 us
where the time goes in v3:
time: 246 us; the launch traced here: 245 us
  Pallas kernels  235 us (96%)
  local copies, waits for them, and re-layouts  8.53 us (3%)
    pallas_call x1, Pallas kernels, gather_weights(): pl.pallas_call(functools.partial(gather_kernel, events), out_shape=(jax.S...  137 us
    pallas_call x1, Pallas kernels, pairs(): pl.pallas_call(pairs_kernel, out_shape=(jax.ShapeDtypeStruct((rows, embed...  69.7 us
    pallas_call x1, Pallas kernels, teacher(): pl.pallas_call(functools.partial(teacher_kernel, steps), out_shape=jax.Sh...  28.5 us
    unnamed x22, local copies, waits for them, and re-layouts  6.42 us

profile of v3, /device:TPU:1, one launch (start us, length us, event | category | flops | bytes accessed | tf_op | source)
XLA Modules:
  0.0 244.8 jit_solution(17065746588800773807)
XLA Ops:
  0.6 0.0 copy-start
  0.6 0.8 copy.20
  1.5 0.1 eq.28
  1.6 0.2 convert_reduce_fusion
  1.8 0.2 fusion
  2.0 0.0 copy-done
  2.0 0.2 convolution_select_fusion
  2.2 0.0 copy-start.3
  2.2 0.9 copy-done.3
  3.1 0.0 copy-start.5
  3.2 0.7 copy-done.5
  3.9 136.5 %gather_weights.1 = (bf16[2,4,4,8,112,896]{5,4,3,2,1,0:T(8,128)(2,1)}, f32[4,1,3584]{2,1,0:T(1,128)S(1)}, f32[256,2,128]{2,1,0:T(2,128)S(1)}) custom-call(bf16[56,1792]{1,0:T(8,128)(2,1)S(1)} %bitcast.16, f32[1,3584]{1,0:T(1,128)S(1)} %copy-done.5, f32[256,2,128]{2,1,0:T(2,128)S(1)} %bitcast.15), custom_call_target="tpu_custom_call" | custom-call | tf_op jit(solution)/shard_map/gather_weights/pallas_call | solution.py:333
  140.4 0.0 copy-start.4
  140.4 0.6 copy-done.4
  141.0 1.3 reshape.48.student_gain_ref
  142.3 0.0 copy-start.7
  142.3 0.0 copy-start.8
  142.3 0.0 copy-start.2
  142.3 0.0 copy-start.6
  142.3 28.5 %teacher_chain.1.embed_ref = bf16[128,1024]{1,0:T(8,128)(2,1)} custom-call(bf16[128,3584]{1,0:T(8,128)(2,1)} %items_ref.1, f32[4,1,3584]{2,1,0:T(1,128)} %copy-done.4, bf16[2,4,32,112,896]{4,3,2,1,0:T(8,128)(2,1)} %bitcast.18, bf16[2,4,32,112,896]{4,3,2,1,0:T(8,128)(2,1)} %bitcast.19, f32[1,3584]{1,0:T(1,128)} %reshape.48.student_gain_ref, ...), custom_call_target="tpu_custom_call" | custom-call | tf_op jit(solution)/shard_map/teacher_chain/pallas_call | solution.py:452
  170.9 0.1 reduce_sum.21
  171.0 0.1 copy.21
  171.1 0.0 copy-done.7
  171.1 0.0 copy-done.8
  171.1 0.1 copy.23.bias_ref
  171.3 0.0 copy-done.2
  171.3 0.0 copy-done.6
  171.3 0.0 copy-start.1
  171.3 0.9 copy-done.1
  172.2 69.7 %pair_exchange.1 = (f32[128,1024]{1,0:T(8,128)S(1)}, f32[256,1024]{1,0:T(8,128)S(1)}, f32[256,128]{1,0:T(8,128)S(1)}) custom-call(s32[2,128]{1,0:T(2,128)S(1)} %add_bitcast_fusion.target_ref, bf16[128,1024]{1,0:T(8,128)(2,1)S(1)} %copy-done.1, f32[512,128]{1,0:T(8,128)S(1)} %bitcast.13, bf16[256,1024]{1,0:T(8,128)(2,1)S(1)} %copy-done.2, ...), custom_call_target="tpu_custom_call" | custom-call | tf_op jit(solution)/shard_map/pair_exchange/pallas_call | solution.py:633
  241.9 0.1 broadcast_in_dim.33
  242.1 0.2 select_reduce_fusion
  242.2 0.2 convert_element_type.13
  242.4 0.6 copy.24
  243.0 0.8 copy.27
  243.8 1.0 copy.28
  (3 shorter events, 0.0 us)
Async XLA Ops:
  0.6 1.3 copy-start
  2.2 0.9 copy-start.3
  3.1 0.7 copy-start.5
  140.4 0.6 copy-start.4
  142.3 28.8 %copy-start.7 = (s32[128,2]{0,1:T(2,128)S(1)}, s32[128,2]{0,1:T(2,128)}, u32[]{:S(2)}) copy-start(s32[128,2]{0,1:T(2,128)} %param.17) | copy-start | bytes 3076
  142.3 28.8 %copy-start.8 = (f32[256]{0:T(256)S(1)}, f32[256]{0:T(256)}, u32[]{:S(2)}) copy-start(f32[256]{0:T(256)} %param.20) | copy-start | bytes 3076
  142.3 28.9 %copy-start.2 = (bf16[256,1024]{1,0:T(8,128)(2,1)S(1)}, bf16[256,1024]{1,0:T(8,128)(2,1)}, u32[]{:S(2)}) copy-start(bf16[256,1024]{1,0:T(8,128)(2,1)} %bank_ref.1) | copy-start | bytes 1572868
  142.3 28.9 %copy-start.6 = (s32[1,128]{1,0:T(1,128)S(1)}, s32[1,128]{1,0:T(1,128)}, u32[]{:S(2)}) copy-start(s32[1,128]{1,0:T(1,128)} %neg_ref.1) | copy-start | bytes 1540
  171.3 1.0 copy-start.1

commit v4 on v3

--- a/solution.py
+++ b/solution.py
@@ -294,6 +294,16 @@
     shares[0].start()
     copies = {}
     pieces = [(begin, min(begin + 32, owners)) for begin in range(1, owners, 32)]
+    newest = []
+
+    def pass_on():
+        for hop in newest:
+            shares.append(share(hop, core, sign))
+            shares[-1].start()
+            if len(shares) > 60 and len(shares) % 16 == 0 and pieces:
+                send_side(*pieces.pop(0))
+        newest.clear()
+
     for kind, hop in events:
         if kind == "start":
             copies[hop] = hop_copy(hop, True)
@@ -301,12 +311,11 @@
         elif kind == "sent":
             copies.pop(hop).wait_send()
         else:
+            pass_on()
             hop_copy(hop, False).wait_recv()
-            if len(shares) > 60 and len(shares) % 16 == 0 and pieces:
-                send_side(*pieces.pop(0))
-            shares.append(share(hop, core, sign))
-            shares[-1].start()
-
+            newest.append(hop)
+
+    pass_on()
     for hop in [None] + plan:
         share(hop, 1 - core, -sign).wait_recv()
     for copy in shares + list(copies.values()):
@@ -591,7 +600,6 @@
     for rank in range(capacity):
         spread = jnp.where(lane == rank, divergence[rank * owners : (rank + 1) * owners], spread)
     kl_out[...] = spread.reshape(owners, 1, lanes)
-    kl_own = exchange(kl_out, kl_home, local_sems.at[1], kl_send, kl_recv)
 
     gap = (valid * (jnp.exp(student_log) - teacher_prob)).astype(BF16)
     for rank in range(capacity):
@@ -600,6 +608,7 @@
             wide[line(rank, split), :] = grad[:, split * lanes : (split + 1) * lanes]
     out_buf[...] = wide[...].reshape(owners, lines, lanes).astype(BF16)
     own = exchange(out_buf, home, local_sems.at[2], back_send, back_recv)
+    kl_own = exchange(kl_out, kl_home, local_sems.at[1], kl_send, kl_recv)
 
     rest = dot(gap, slots[...], ((0,), (0,))) * score_scale
     bank_grad = jnp.zeros(bank_grad_ref.shape, F32)

time: 246 us -> 246 us (level)
  no operation moved by 1% of the time
where the time goes in v4:
time: 246 us; the launch traced here: 245 us
  Pallas kernels  235 us (96%)
  local copies, waits for them, and re-layouts  8.53 us (3%)
    pallas_call x1, Pallas kernels, gather_weights(): pl.pallas_call(functools.partial(gather_kernel, events), out_shape=(jax.S...  136 us
    pallas_call x1, Pallas kernels, pairs(): pl.pallas_call(pairs_kernel, out_shape=(jax.ShapeDtypeStruct((rows, embed...  70.4 us
    pallas_call x1, Pallas kernels, teacher(): pl.pallas_call(functools.partial(teacher_kernel, steps), out_shape=jax.Sh...  28.5 us
    unnamed x22, local copies, waits for them, and re-layouts  6.42 us

profile of v4, /device:TPU:1, one launch (start us, length us, event | category | flops | bytes accessed | tf_op | source)
XLA Modules:
  0.0 245.4 jit_solution(5691708908293523134)
XLA Ops:
  0.6 0.0 copy-start
  0.6 0.8 copy.20
  1.5 0.1 eq.28
  1.6 0.2 convert_reduce_fusion
  1.8 0.2 fusion
  2.0 0.0 copy-done
  2.0 0.2 convolution_select_fusion
  2.2 0.0 copy-start.3
  2.2 0.9 copy-done.3
  3.1 0.0 copy-start.5
  3.2 0.7 copy-done.5
  3.9 136.4 %gather_weights.1 = (bf16[2,4,4,8,112,896]{5,4,3,2,1,0:T(8,128)(2,1)}, f32[4,1,3584]{2,1,0:T(1,128)S(1)}, f32[256,2,128]{2,1,0:T(2,128)S(1)}) custom-call(bf16[56,1792]{1,0:T(8,128)(2,1)S(1)} %bitcast.16, f32[1,3584]{1,0:T(1,128)S(1)} %copy-done.5, f32[256,2,128]{2,1,0:T(2,128)S(1)} %bitcast.15), custom_call_target="tpu_custom_call" | custom-call | tf_op jit(solution)/shard_map/gather_weights/pallas_call | solution.py:342
  140.3 0.0 copy-start.4
  140.3 0.6 copy-done.4
  140.9 1.3 reshape.48.student_gain_ref
  142.3 0.0 copy-start.7
  142.3 0.0 copy-start.8
  142.3 0.0 copy-start.2
  142.3 0.0 copy-start.6
  142.3 28.5 %teacher_chain.1.embed_ref = bf16[128,1024]{1,0:T(8,128)(2,1)} custom-call(bf16[128,3584]{1,0:T(8,128)(2,1)} %items_ref.1, f32[4,1,3584]{2,1,0:T(1,128)} %copy-done.4, bf16[2,4,32,112,896]{4,3,2,1,0:T(8,128)(2,1)} %bitcast.18, bf16[2,4,32,112,896]{4,3,2,1,0:T(8,128)(2,1)} %bitcast.19, f32[1,3584]{1,0:T(1,128)} %reshape.48.student_gain_ref, ...), custom_call_target="tpu_custom_call" | custom-call | tf_op jit(solution)/shard_map/teacher_chain/pallas_call | solution.py:461
  170.8 0.1 reduce_sum.21
  171.0 0.1 copy.21
  171.0 0.0 copy-done.7
  171.0 0.0 copy-done.8
  171.1 0.1 copy.23.bias_ref
  171.2 0.0 copy-done.2
  171.2 0.0 copy-done.6
  171.2 0.0 copy-start.1
  171.2 0.9 copy-done.1
  172.2 70.4 %pair_exchange.1 = (f32[128,1024]{1,0:T(8,128)S(1)}, f32[256,1024]{1,0:T(8,128)S(1)}, f32[256,128]{1,0:T(8,128)S(1)}) custom-call(s32[2,128]{1,0:T(2,128)S(1)} %add_bitcast_fusion.target_ref, bf16[128,1024]{1,0:T(8,128)(2,1)S(1)} %copy-done.1, f32[512,128]{1,0:T(8,128)S(1)} %bitcast.13, bf16[256,1024]{1,0:T(8,128)(2,1)S(1)} %copy-done.2, ...), custom_call_target="tpu_custom_call" | custom-call | tf_op jit(solution)/shard_map/pair_exchange/pallas_call | solution.py:642
  242.6 0.1 broadcast_in_dim.33
  242.7 0.2 select_reduce_fusion
  242.9 0.2 convert_element_type.13
  243.1 0.6 copy.24
  243.7 0.8 copy.27
  244.5 1.0 copy.28
  (3 shorter events, 0.0 us)
Async XLA Ops:
  0.6 1.3 copy-start
  2.2 0.9 copy-start.3
  3.1 0.7 copy-start.5
  140.3 0.6 copy-start.4
  142.3 28.8 %copy-start.7 = (s32[128,2]{0,1:T(2,128)S(1)}, s32[128,2]{0,1:T(2,128)}, u32[]{:S(2)}) copy-start(s32[128,2]{0,1:T(2,128)} %param.17) | copy-start | bytes 3076
  142.3 28.8 %copy-start.8 = (f32[256]{0:T(256)S(1)}, f32[256]{0:T(256)}, u32[]{:S(2)}) copy-start(f32[256]{0:T(256)} %param.20) | copy-start | bytes 3076
  142.3 28.9 %copy-start.2 = (bf16[256,1024]{1,0:T(8,128)(2,1)S(1)}, bf16[256,1024]{1,0:T(8,128)(2,1)}, u32[]{:S(2)}) copy-start(bf16[256,1024]{1,0:T(8,128)(2,1)} %bank_ref.1) | copy-start | bytes 1572868
  142.3 28.9 %copy-start.6 = (s32[1,128]{1,0:T(1,128)S(1)}, s32[1,128]{1,0:T(1,128)}, u32[]{:S(2)}) copy-start(s32[1,128]{1,0:T(1,128)} %neg_ref.1) | copy-start | bytes 1540
  171.2 1.0 copy-start.1

commit v5 on v4

--- a/solution.py
+++ b/solution.py
@@ -232,7 +232,6 @@
 
     mine = pltpu.make_async_copy(block, out_ref.at[core, x, y, z], local_sem)
     mine.start()
-    mine.wait()
 
     starts = [sum(PART_ROWS[:part]) for part in range(len(PART_ROWS))]
     plan = [hop for kind, hop in events if kind == "came"]
@@ -256,8 +255,10 @@
         ref = held(hop, k - step if sending else k, core, sign)
         to = list(here)
         to[axis] = reach(axis, step, sign)
+        fresh = sending and k == step and not any(j is None or j for j in hop[3])
+        rows_of = pl.ds(starts[part], PART_ROWS[part])
         return pltpu.make_async_remote_copy(
-            src_ref=ref,
+            src_ref=block.at[rows_of, :] if fresh else ref,
             dst_ref=ref,
             send_sem=send_sem.at[number[hop]],
             recv_sem=recv_sem.at[number[hop]],
@@ -269,7 +270,7 @@
         ref = out_ref.at[on, x, y, z] if hop is None else held(hop, hop[2], on, way)
         index = len(plan) if hop is None else number[hop]
         return pltpu.make_async_remote_copy(
-            src_ref=ref,
+            src_ref=block if hop is None else ref,
             dst_ref=ref,
             send_sem=sib_send.at[index],
             recv_sem=sib_recv.at[index],
@@ -312,6 +313,8 @@
             copies.pop(hop).wait_send()
         else:
             pass_on()
+            if hop == plan[0]:
+                mine.wait()
             hop_copy(hop, False).wait_recv()
             newest.append(hop)
 
@@ -419,21 +422,29 @@
     right = right_ref[0, 0].reshape(depth, half)
     place = pl.ds(pl.multiple_of(chunk * depth, HD), depth)
 
+    cut = half // 256 * 256
+    seam = 2 * (half - cut)
+    middle = jnp.concatenate([left[:, cut:], right[:, : half - cut]], axis=1)
+    pieces = (
+        (slice(0, cut), left[:, :cut]),
+        (slice(cut, cut + seam), middle),
+        (slice(cut + seam, width), right[:, half - cut :]),
+    )
+
     @pl.when(begins & is_value)
     def _():
-        total[:, :half] = dot(act[:, :depth], left)
-        total[:, half:width] = dot(act[:, :depth], right)
+        for cols, piece in pieces:
+            total[:, cols] = dot(act[:, :depth], piece)
 
     @pl.when((chunk > 0) & is_value)
     def _():
-        total[:, :half] += dot(act[:, place], left)
-        total[:, half:width] += dot(act[:, place], right)
+        for cols, piece in pieces:
+            total[:, cols] += dot(act[:, place], piece)
 
     @pl.when(is_output)
     def _():
-        total[:, place] = dot(act[:, :half], left, ((1,), (1,))) + dot(
-            act[:, half:width], right, ((1,), (1,))
-        )
+        parts = [dot(act[:, cols], piece, ((1,), (1,))) for cols, piece in pieces]
+        total[:, place] = parts[0] + parts[1] + parts[2]
 
     @pl.when(step == pl.num_programs(0) - 1)
     def _():

time: 246 us -> 244 us (level)
  no operation moved by 1% of the time
where the time goes in v5:
time: 244 us
  Pallas kernels  234 us (96%)
  local copies, waits for them, and re-layouts  8.53 us (3%)
    pallas_call x1, Pallas kernels, gather_weights(): pl.pallas_call(functools.partial(gather_kernel, events), out_shape=(jax.S...  136 us
    pallas_call x1, Pallas kernels, pairs(): pl.pallas_call(pairs_kernel, out_shape=(jax.ShapeDtypeStruct((rows, embed...  70.2 us
    pallas_call x1, Pallas kernels, teacher(): pl.pallas_call(functools.partial(teacher_kernel, steps), out_shape=jax.Sh...  28.3 us
    unnamed x22, local copies, waits for them, and re-layouts  6.42 us

profile of v5, /device:TPU:1, one launch (start us, length us, event | category | flops | bytes accessed | tf_op | source)
XLA Modules:
  0.0 244.1 jit_solution(2358024496769902981)
XLA Ops:
  0.6 0.0 copy-start
  0.6 0.8 copy.20
  1.5 0.1 eq.28
  1.6 0.2 convert_reduce_fusion
  1.8 0.2 fusion
  2.0 0.0 copy-done
  2.0 0.2 convolution_select_fusion
  2.2 0.0 copy-start.3
  2.2 0.9 copy-done.3
  3.1 0.0 copy-start.5
  3.2 0.7 copy-done.5
  3.9 135.6 %gather_weights.1 = (bf16[2,4,4,8,112,896]{5,4,3,2,1,0:T(8,128)(2,1)}, f32[4,1,3584]{2,1,0:T(1,128)S(1)}, f32[256,2,128]{2,1,0:T(2,128)S(1)}) custom-call(bf16[56,1792]{1,0:T(8,128)(2,1)S(1)} %bitcast.16, f32[1,3584]{1,0:T(1,128)S(1)} %copy-done.5, f32[256,2,128]{2,1,0:T(2,128)S(1)} %bitcast.15), custom_call_target="tpu_custom_call" | custom-call | tf_op jit(solution)/shard_map/gather_weights/pallas_call | solution.py:345
  139.4 0.0 copy-start.4
  139.4 0.6 copy-done.4
  140.1 1.3 reshape.48.student_gain_ref
  141.4 0.0 copy-start.7
  141.4 0.0 copy-start.8
  141.4 0.0 copy-start.2
  141.4 0.0 copy-start.6
  141.4 28.3 %teacher_chain.1.embed_ref = bf16[128,1024]{1,0:T(8,128)(2,1)} custom-call(bf16[128,3584]{1,0:T(8,128)(2,1)} %items_ref.1, f32[4,1,3584]{2,1,0:T(1,128)} %copy-done.4, bf16[2,4,32,112,896]{4,3,2,1,0:T(8,128)(2,1)} %bitcast.18, bf16[2,4,32,112,896]{4,3,2,1,0:T(8,128)(2,1)} %bitcast.19, f32[1,3584]{1,0:T(1,128)} %reshape.48.student_gain_ref, ...), custom_call_target="tpu_custom_call" | custom-call | tf_op jit(solution)/shard_map/teacher_chain/pallas_call | solution.py:472
  169.7 0.1 reduce_sum.21
  169.9 0.1 copy.21
  169.9 0.0 copy-done.7
  169.9 0.0 copy-done.8
  170.0 0.1 copy.23.bias_ref
  170.1 0.0 copy-done.2
  170.1 0.0 copy-done.6
  170.1 0.0 copy-start.1
  170.1 0.9 copy-done.1
  171.1 70.2 %pair_exchange.1 = (f32[128,1024]{1,0:T(8,128)S(1)}, f32[256,1024]{1,0:T(8,128)S(1)}, f32[256,128]{1,0:T(8,128)S(1)}) custom-call(s32[2,128]{1,0:T(2,128)S(1)} %add_bitcast_fusion.target_ref, bf16[128,1024]{1,0:T(8,128)(2,1)S(1)} %copy-done.1, f32[512,128]{1,0:T(8,128)S(1)} %bitcast.13, bf16[256,1024]{1,0:T(8,128)(2,1)S(1)} %copy-done.2, ...), custom_call_target="tpu_custom_call" | custom-call | tf_op jit(solution)/shard_map/pair_exchange/pallas_call | solution.py:653
  241.3 0.1 broadcast_in_dim.33
  241.4 0.2 select_reduce_fusion
  241.6 0.2 convert_element_type.13
  241.7 0.6 copy.24
  242.4 0.8 copy.27
  243.1 1.0 copy.28
  (3 shorter events, 0.0 us)
Async XLA Ops:
  0.6 1.3 copy-start
  2.2 0.9 copy-start.3
  3.1 0.7 copy-start.5
  139.4 0.6 copy-start.4
  141.4 28.5 %copy-start.7 = (s32[128,2]{0,1:T(2,128)S(1)}, s32[128,2]{0,1:T(2,128)}, u32[]{:S(2)}) copy-start(s32[128,2]{0,1:T(2,128)} %param.17) | copy-start | bytes 3076
  141.4 28.6 %copy-start.8 = (f32[256]{0:T(256)S(1)}, f32[256]{0:T(256)}, u32[]{:S(2)}) copy-start(f32[256]{0:T(256)} %param.20) | copy-start | bytes 3076
  141.4 28.7 %copy-start.2 = (bf16[256,1024]{1,0:T(8,128)(2,1)S(1)}, bf16[256,1024]{1,0:T(8,128)(2,1)}, u32[]{:S(2)}) copy-start(bf16[256,1024]{1,0:T(8,128)(2,1)} %bank_ref.1) | copy-start | bytes 1572868
  141.4 28.7 %copy-start.6 = (s32[1,128]{1,0:T(1,128)S(1)}, s32[1,128]{1,0:T(1,128)}, u32[]{:S(2)}) copy-start(s32[1,128]{1,0:T(1,128)} %neg_ref.1) | copy-start | bytes 1540
  170.1 1.0 copy-start.1
